TPU v7x, 32 devices: a whole 2x2x4 slice. The times are simulated.
32 devices in a mesh: space: 8 (over z, x), vel: 4 (over y, core).
Axes of the slice: x: 2, y: 2, z: 4, core: 2. Of those that a mesh axis runs over, the one named last changes fastest.
Arguments:
- distribution: float32 [32, 32, 2, 4096], P('space', None, None, 'vel'), may hold values from 0.0004 to 1, as said below
- wall_mask: int32 [32, 2, 2], P('space'), may hold values 0 or 1
- grid_point: int32 [4096], P('vel'), may hold values from 0 to 4095, as said below
- mirror_slot: int32 [4096], P('vel'), may hold values from 0 to 4095, as said below
Outputs:
- swept: float32 [32, 32, 2, 4096], P('space', None, None, 'vel')
Inputs may be any that keep to these rules, and one draw needn't show every extreme that they name: grid_point is a permutation of 0 .. 4095. mirror_slot is a permutation; slot mirror_slot[s] holds the velocity of slot s with its second component negated. `distribution`: every entry is positive.
All inputs are finite; a program needn't handle non-finite values. No bound on the sum of `wall_mask` on one device may be relied on, other than what follows from the above.
Results may differ from a plain program's by a relative error of at most 0.0003.
Values sent between devices are 32-bit elements; how exact they have to be, the bound alone decides.
A program may use at most 64 MiB of HBM per device.

v0:
```python
import math

import jax
import jax.numpy as jnp
from jax import lax
from jax.sharding import PartitionSpec as P

VS = 16


stream_x = 40.0
stream_y = 0.15
stream_z = 0.05
relaxation_multiplier = 0.05
shear_power_index = 0.81
diffusivity_ratio = 2.0 / 3.0


def passed_along(x, axis, by):
    size = lax.axis_size(axis)
    pairs = [(i, i + by) for i in range(size) if 0 <= i + by < size]
    return lax.ppermute(x, axis, pairs)


def velocity_table(grid_point, side):
    spacing = 8.0 / side
    half = (side - 1) / 2.0
    first = (grid_point // (side * side)).astype(jnp.float32)
    quadratic_average = (grid_point // side % side).astype(jnp.float32)
    third = (grid_point % side).astype(jnp.float32)
    return jnp.stack(
        [(first - half) * spacing, (quadratic_average - half) * spacing, (third - half) * spacing]
    )


def velocity_sums(table, flat, integration_coefficient):
    return integration_coefficient * lax.dot_general(
        table,
        flat,
        (((1,), (1,)), ((), ())),
        precision=lax.Precision.HIGHEST,
        preferred_element_type=jnp.float32,
    )


def compose(earlier, later):
    return (later[0] * earlier[0], later[0] * earlier[1] + later[1])


def shards(distribution, wall_mask, grid_point, mirror_slot):
    integration_coefficient = (8.0 / VS) ** 3
    xi = velocity_table(grid_point, VS)
    depth, rows, planes, width = distribution.shape
    cells = depth * rows * planes
    flat = distribution.reshape(cells, width)
    wall_rows = jnp.stack([distribution[:, 0], distribution[:, rows - 1]], axis=1)
    gathered = lax.all_gather(wall_rows, "vel", axis=3, tiled=True)
    mirrored = jnp.take(gathered, mirror_slot, axis=3)
    unity = jnp.ones_like(xi[0])
    norm_sq = xi[0] * xi[0] + xi[1] * xi[1] + xi[2] * xi[2]
    raw_table = jnp.stack(
        [
            unity,
            xi[0],
            xi[1],
            xi[2],
            xi[0] * xi[0],
            xi[1] * xi[1],
            xi[2] * xi[2],
            xi[0] * xi[1],
            xi[0] * xi[2],
            xi[1] * xi[2],
            xi[0] * norm_sq,
            xi[1] * norm_sq,
            xi[2] * norm_sq,
        ]
    )
    raw = lax.psum(velocity_sums(raw_table, flat, integration_coefficient), "vel")
    particle_concentration = raw[0]
    momentum = raw[1:4]
    flow = momentum / particle_concentration[None]
    tensor = [[raw[4], raw[7], raw[8]], [raw[7], raw[5], raw[9]], [raw[8], raw[9], raw[6]]]
    trace_sum = raw[4] + raw[5] + raw[6]
    flow_sq = flow[0] * flow[0] + flow[1] * flow[1] + flow[2] * flow[2]
    kinetic_heat_level = (trace_sum - particle_concentration * flow_sq) / (
        3.0 * particle_concentration
    )
    flow_mom = flow[0] * momentum[0] + flow[1] * momentum[1] + flow[2] * momentum[2]
    heat_rows = []
    for k in range(3):
        contracted = flow[0] * tensor[k][0] + flow[1] * tensor[k][1] + flow[2] * tensor[k][2]
        heat_rows.append(
            0.5
            * (
                raw[10 + k]
                - 2.0 * contracted
                + flow_sq * momentum[k]
                - flow[k] * trace_sum
                + 2.0 * flow[k] * flow_mom
                - flow[k] * flow_sq * particle_concentration
            )
        )
    heat = jnp.stack(heat_rows)
    peculiar = xi[:, None, :] - flow[:, :, None]
    magnitude_square = jnp.sum(peculiar * peculiar, axis=0)
    thermal_level_group = kinetic_heat_level[:, None]
    particle_concentration_local = particle_concentration[:, None]
    gaussian_equilibrium = (
        particle_concentration_local
        / (2.0 * math.pi * thermal_level_group) ** 1.5
        * jnp.exp(-magnitude_square / (2.0 * thermal_level_group))
    )
    lengthwise = (
        peculiar[0] * heat[0][:, None]
        + peculiar[1] * heat[1][:, None]
        + peculiar[2] * heat[2][:, None]
    )
    corrected_equilibrium = gaussian_equilibrium * (
        1.0
        + (1.0 - diffusivity_ratio)
        * lengthwise
        / (5.0 * particle_concentration_local * thermal_level_group * thermal_level_group)
        * (magnitude_square / thermal_level_group - 5.0)
    )
    relaxation_frequency = (
        relaxation_multiplier
        * particle_concentration
        * kinetic_heat_level ** (1.0 - shear_power_index)
    )
    corrected_equilibrium = corrected_equilibrium.reshape(depth, rows, planes, width)
    relaxation_frequency = relaxation_frequency.reshape(depth, rows, planes, 1)
    ghost_low = jnp.where(
        wall_mask[:, 0, :, None] == 1, mirrored[:, 0], corrected_equilibrium[:, 0]
    )
    ghost_high = jnp.where(
        wall_mask[:, 1, :, None] == 1, mirrored[:, 1], corrected_equilibrium[:, rows - 1]
    )
    padded = jnp.concatenate([ghost_low[:, None], distribution, ghost_high[:, None]], axis=1)
    below = padded[:, :-2]
    above = padded[:, 2:]
    y_flux = xi[1] * jnp.where(xi[1] > 0, distribution - below, above - distribution)
    z_flux = xi[2] * jnp.where(
        xi[2] > 0,
        distribution - jnp.roll(distribution, 1, axis=2),
        jnp.roll(distribution, -1, axis=2) - distribution,
    )
    sigma = stream_x * jnp.abs(xi[0])
    denom = 1.0 + sigma + relaxation_frequency
    coef_a = sigma / denom
    coef_b = (
        distribution
        + relaxation_frequency * corrected_equilibrium
        - stream_y * y_flux
        - stream_z * z_flux
    ) / denom
    first_block = lax.axis_index("space") == 0
    last_block = lax.axis_index("space") == lax.axis_size("space") - 1
    down_a = coef_a.at[0].set(jnp.where(first_block, 0.0, coef_a[0]))
    down_b = coef_b.at[0].set(
        jnp.where(first_block, coef_b[0] + coef_a[0] * corrected_equilibrium[0], coef_b[0])
    )
    up_a = coef_a.at[depth - 1].set(jnp.where(last_block, 0.0, coef_a[depth - 1]))
    up_b = coef_b.at[depth - 1].set(
        jnp.where(
            last_block,
            coef_b[depth - 1] + coef_a[depth - 1] * corrected_equilibrium[depth - 1],
            coef_b[depth - 1],
        )
    )
    down_a, down_b = lax.associative_scan(compose, (down_a, down_b), axis=0)
    flip_a, flip_b = lax.associative_scan(compose, (jnp.flip(up_a, 0), jnp.flip(up_b, 0)), axis=0)
    up_a = jnp.flip(flip_a, 0)
    up_b = jnp.flip(flip_b, 0)
    block_down = (down_a[depth - 1], down_b[depth - 1])
    block_up = (up_a[0], up_b[0])

    def relay_step(step, faces):
        out_down = block_down[0] * faces[0] + block_down[1]
        out_up = block_up[0] * faces[1] + block_up[1]
        return (passed_along(out_down, "space", 1), passed_along(out_up, "space", -1))

    zero_face = jnp.zeros_like(block_down[1])
    enter_down, enter_up = lax.fori_loop(
        0, lax.axis_size("space") - 1, relay_step, (zero_face, zero_face)
    )
    downstream = down_a * enter_down[None] + down_b
    upstream = up_a * enter_up[None] + up_b
    return jnp.where(xi[0] > 0, downstream, upstream)


def solution(mesh):
    placed = (P("space", None, None, "vel"), P("space", None, None), P("vel"), P("vel"))
    return jax.shard_map(
        shards, mesh=mesh, in_specs=placed, out_specs=P("space", None, None, "vel"), check_vma=False
    )
```

profile of v0, /device:TPU:0, one launch (start us, length us, event | category | flops | bytes accessed | tf_op | source)
XLA Modules:
  0.0 267.4 jit_solution(5053530969670408959)
XLA Ops:
  4.9 12.7 %psum.7 = f32[13,256]{1,0:T(8,128)S(1)} all-reduce(f32[13,256]{1,0:T(8,128)S(1)} %convolution_multiply_fusion), channel_id=1, replica_groups=mesh['space'=8,'vel'=4] {'vel'}, use_global_device_ids=true, to_apply=%region_0.1 | all-reduce | flops 3328 | bytes 26624 | tf_op jit(solution)/shard_map/psum | solution.py:78
  35.8 4.4 %fusion.19 = f32[4,32,2,1024]{3,1,2,0:T(8,128)} fusion(f32[4,32,2,1024]{3,2,1,0:T(2,128)} %squeeze.174, f32[4,32,2,1024]{3,2,1,0:T(2,128)} %squeeze.171, f32[4,32,2,1024]{3,2,1,0:T(2,128)S(1)} %squeeze.164, f32[4,32,2,1024]{3,2,1,0:T(2,128)} %reduce_sum.12, f32[4,32,2]{1,2,0:T(2,128)S(1)} %copy.404, f32[4,32,2]{1,2,0:T(2,128)S(1)} %copy.403, ...), kind=kLoop, calls=%fused_computation.34 | loop fusion | flops 3932160 | bytes 5250048 | tf_op jit(solution)/shard_map/mul | solution.py:118
  41.5 49.5 %all_gather.3 = f32[4,2,2,4096]{0,2,3,1:T(2,128)} all-gather(f32[4,2,2,1024]{0,2,3,1:T(2,128)S(1)} %copy.410), channel_id=1, replica_groups=mesh['space'=8,'vel'=4] {'vel'}, dimensions={3}, use_global_device_ids=true | all-gather | bytes 327680 | tf_op jit(solution)/shard_map/all_gather | solution.py:57
  91.0 8.1 %gather_fusion = f32[1024,4,2,2]{1,3,2,0:T(2,128)S(1)} fusion(f32[4,2,2,4096]{0,2,3,1:T(2,128)} %all_gather.3, s32[1024]{0:T(1024)S(1)} %fusion.48), kind=kCustom, calls=%fused_computation | custom fusion | bytes 135168 | tf_op jit(solution)/shard_map/jit(_take)/gather | solution.py:58
  113.5 4.1 %pad.75 = f32[4,32,2,1024]{3,1,2,0:T(8,128)} pad(f32[2,32,2,1024]{3,1,2,0:T(8,128)} %get-tuple-element.286, f32[]{:T(128)} %constant.187.clone.1), padding=1_0_1x0_0_0x0_0_0x0_0_0 | pad | bytes 1572868 | tf_op jit(solution)/shard_map/pad | solution.py:171
  132.5 4.1 %pad.67 = f32[4,32,2,1024]{3,1,2,0:T(8,128)} pad(f32[2,32,2,1024]{3,1,2,0:T(8,128)} %get-tuple-element.288, f32[]{:T(128)} %constant.187.clone.1), padding=1_0_1x0_0_0x0_0_0x0_0_0 | pad | bytes 1572868 | tf_op jit(solution)/shard_map/pad | solution.py:170
  142.3 4.2 %pad.62 = f32[4,32,2,1024]{3,1,2,0:T(8,128)} pad(f32[2,32,2,1024]{3,1,2,0:T(8,128)} %get-tuple-element.284, f32[]{:T(128)} %constant.187.clone.1), padding=0_1_1x0_0_0x0_0_0x0_0_0 | pad | bytes 1572868 | tf_op jit(solution)/shard_map/pad | solution.py:170
  147.8 113.8 %while.16 = (s32[]{:T(128)}, f32[32,2,1024]{2,1,0:T(2,128)S(1)}, f32[32,2,1024]{2,1,0:T(2,128)S(1)}, f32[32,2,1024]{2,1,0:T(2,128)S(1)}, f32[32,2,1024]{2,1,0:T(...) while((s32[]{:T(128)}, f32[32,2,1024]{2,1,0:T(2,128)S(1)}, ...), condition=%wide.region_3.4_spmd, body=%wide.region_2.3_spmd.sunk | while | flops 262146 | bytes 4194469 | solution.py:183
  147.9 3.5 %collective-permute-start = (f32[32,2,1024]{2,1,0:T(2,128)S(1)}, f32[32,2,1024]{2,1,0:T(2,128)S(1)}, u32[]{:S(2)}, u32[]{:S(2)}) collective-permute-start(f32[32,2,1024]{2,1,0:T(2,128)S(1)} %bitcast.96), channel_id=1, source_target_pairs={{0,4},{4,8},{8,12},{12,16},{16,20},{20,24},{24,28},{1,5},{5,9},{9,... | collective-permute-start | bytes 786440 | tf_op jit(solution)/shard_map/while/body/eval_jaxpr/ppermute | solution.py:22
  152.8 10.3 %collective-permute-done = f32[32,2,1024]{2,1,0:T(2,128)S(1)} collective-permute-done((f32[32,2,1024]{2,1,0:T(2,128)S(1)}, f32[32,2,1024]{2,1,0:T(2,128)S(1)}, u32[]{:S(2)}, u32[]{:S(2)}) %collective-permute-start) | collective-permute-done | bytes 262176 | tf_op jit(solution)/shard_map/while/body/eval_jaxpr/ppermute | solution.py:22
  163.1 4.4 %collective-permute-start = (f32[32,2,1024]{2,1,0:T(2,128)S(1)}, f32[32,2,1024]{2,1,0:T(2,128)S(1)}, u32[]{:S(2)}, u32[]{:S(2)}) collective-permute-start(f32[32,2,1024]{2,1,0:T(2,128)S(1)} %bitcast.96), channel_id=1, source_target_pairs={{0,4},{4,8},{8,12},{12,16},{16,20},{20,24},{24,28},{1,5},{5,9},{9,... | collective-permute-start | bytes 786440 | tf_op jit(solution)/shard_map/while/body/eval_jaxpr/ppermute | solution.py:22
  168.9 4.0 %collective-permute-done = f32[32,2,1024]{2,1,0:T(2,128)S(1)} collective-permute-done((f32[32,2,1024]{2,1,0:T(2,128)S(1)}, f32[32,2,1024]{2,1,0:T(2,128)S(1)}, u32[]{:S(2)}, u32[]{:S(2)}) %collective-permute-start) | collective-permute-done | bytes 262176 | tf_op jit(solution)/shard_map/while/body/eval_jaxpr/ppermute | solution.py:22
  172.9 5.3 %collective-permute-done.1 = f32[32,2,1024]{2,1,0:T(2,128)S(1)} collective-permute-done((f32[32,2,1024]{2,1,0:T(2,128)S(1)}, f32[32,2,1024]{2,1,0:T(2,128)S(1)}, u32[]{:S(2)}, u32[]{:S(2)}) %collective-permute-start.1) | collective-permute-done | bytes 262176 | tf_op jit(solution)/shard_map/while/body/eval_jaxpr/ppermute | solution.py:22
  178.2 4.7 %collective-permute-start = (f32[32,2,1024]{2,1,0:T(2,128)S(1)}, f32[32,2,1024]{2,1,0:T(2,128)S(1)}, u32[]{:S(2)}, u32[]{:S(2)}) collective-permute-start(f32[32,2,1024]{2,1,0:T(2,128)S(1)} %bitcast.96), channel_id=1, source_target_pairs={{0,4},{4,8},{8,12},{12,16},{16,20},{20,24},{24,28},{1,5},{5,9},{9,... | collective-permute-start | bytes 786440 | tf_op jit(solution)/shard_map/while/body/eval_jaxpr/ppermute | solution.py:22
  187.4 7.4 %collective-permute-done.1 = f32[32,2,1024]{2,1,0:T(2,128)S(1)} collective-permute-done((f32[32,2,1024]{2,1,0:T(2,128)S(1)}, f32[32,2,1024]{2,1,0:T(2,128)S(1)}, u32[]{:S(2)}, u32[]{:S(2)}) %collective-permute-start.1) | collective-permute-done | bytes 262176 | tf_op jit(solution)/shard_map/while/body/eval_jaxpr/ppermute | solution.py:22
  194.9 4.6 %collective-permute-start = (f32[32,2,1024]{2,1,0:T(2,128)S(1)}, f32[32,2,1024]{2,1,0:T(2,128)S(1)}, u32[]{:S(2)}, u32[]{:S(2)}) collective-permute-start(f32[32,2,1024]{2,1,0:T(2,128)S(1)} %bitcast.96), channel_id=1, source_target_pairs={{0,4},{4,8},{8,12},{12,16},{16,20},{20,24},{24,28},{1,5},{5,9},{9,... | collective-permute-start | bytes 786440 | tf_op jit(solution)/shard_map/while/body/eval_jaxpr/ppermute | solution.py:22
  200.8 3.2 %collective-permute-done = f32[32,2,1024]{2,1,0:T(2,128)S(1)} collective-permute-done((f32[32,2,1024]{2,1,0:T(2,128)S(1)}, f32[32,2,1024]{2,1,0:T(2,128)S(1)}, u32[]{:S(2)}, u32[]{:S(2)}) %collective-permute-start) | collective-permute-done | bytes 262176 | tf_op jit(solution)/shard_map/while/body/eval_jaxpr/ppermute | solution.py:22
  204.0 7.5 %collective-permute-done.1 = f32[32,2,1024]{2,1,0:T(2,128)S(1)} collective-permute-done((f32[32,2,1024]{2,1,0:T(2,128)S(1)}, f32[32,2,1024]{2,1,0:T(2,128)S(1)}, u32[]{:S(2)}, u32[]{:S(2)}) %collective-permute-start.1) | collective-permute-done | bytes 262176 | tf_op jit(solution)/shard_map/while/body/eval_jaxpr/ppermute | solution.py:22
  211.6 4.6 %collective-permute-start = (f32[32,2,1024]{2,1,0:T(2,128)S(1)}, f32[32,2,1024]{2,1,0:T(2,128)S(1)}, u32[]{:S(2)}, u32[]{:S(2)}) collective-permute-start(f32[32,2,1024]{2,1,0:T(2,128)S(1)} %bitcast.96), channel_id=1, source_target_pairs={{0,4},{4,8},{8,12},{12,16},{16,20},{20,24},{24,28},{1,5},{5,9},{9,... | collective-permute-start | bytes 786440 | tf_op jit(solution)/shard_map/while/body/eval_jaxpr/ppermute | solution.py:22
  220.7 7.5 %collective-permute-done.1 = f32[32,2,1024]{2,1,0:T(2,128)S(1)} collective-permute-done((f32[32,2,1024]{2,1,0:T(2,128)S(1)}, f32[32,2,1024]{2,1,0:T(2,128)S(1)}, u32[]{:S(2)}, u32[]{:S(2)}) %collective-permute-start.1) | collective-permute-done | bytes 262176 | tf_op jit(solution)/shard_map/while/body/eval_jaxpr/ppermute | solution.py:22
  228.3 4.6 %collective-permute-start = (f32[32,2,1024]{2,1,0:T(2,128)S(1)}, f32[32,2,1024]{2,1,0:T(2,128)S(1)}, u32[]{:S(2)}, u32[]{:S(2)}) collective-permute-start(f32[32,2,1024]{2,1,0:T(2,128)S(1)} %bitcast.96), channel_id=1, source_target_pairs={{0,4},{4,8},{8,12},{12,16},{16,20},{20,24},{24,28},{1,5},{5,9},{9,... | collective-permute-start | bytes 786440 | tf_op jit(solution)/shard_map/while/body/eval_jaxpr/ppermute | solution.py:22
  237.4 7.5 %collective-permute-done.1 = f32[32,2,1024]{2,1,0:T(2,128)S(1)} collective-permute-done((f32[32,2,1024]{2,1,0:T(2,128)S(1)}, f32[32,2,1024]{2,1,0:T(2,128)S(1)}, u32[]{:S(2)}, u32[]{:S(2)}) %collective-permute-start.1) | collective-permute-done | bytes 262176 | tf_op jit(solution)/shard_map/while/body/eval_jaxpr/ppermute | solution.py:22
  244.9 4.6 %collective-permute-start = (f32[32,2,1024]{2,1,0:T(2,128)S(1)}, f32[32,2,1024]{2,1,0:T(2,128)S(1)}, u32[]{:S(2)}, u32[]{:S(2)}) collective-permute-start(f32[32,2,1024]{2,1,0:T(2,128)S(1)} %bitcast.96), channel_id=1, source_target_pairs={{0,4},{4,8},{8,12},{12,16},{16,20},{20,24},{24,28},{1,5},{5,9},{9,... | collective-permute-start | bytes 786440 | tf_op jit(solution)/shard_map/while/body/eval_jaxpr/ppermute | solution.py:22
  254.1 7.5 %collective-permute-done.1 = f32[32,2,1024]{2,1,0:T(2,128)S(1)} collective-permute-done((f32[32,2,1024]{2,1,0:T(2,128)S(1)}, f32[32,2,1024]{2,1,0:T(2,128)S(1)}, u32[]{:S(2)}, u32[]{:S(2)}) %collective-permute-start.1) | collective-permute-done | bytes 262176 | tf_op jit(solution)/shard_map/while/body/eval_jaxpr/ppermute | solution.py:22
  (216 shorter events, 88.1 us)
Async XLA Ops:
  27.8 4.8 %copy-start.13 = (f32[1,256,1024]{2,1,0:T(8,128)S(1)}, f32[1,256,1024]{2,1,0:T(8,128)}, u32[]{:S(2)}) copy-start(f32[1,256,1024]{2,1,0:T(8,128)} %get-tuple-element.187) | copy-start | bytes 3145732
  27.8 6.4 %copy-start.1 = (f32[256,1024]{1,0:T(8,128)S(1)}, f32[256,1024]{1,0:T(8,128)}, u32[]{:S(2)}) copy-start(f32[256,1024]{1,0:T(8,128)} %copy-done) | copy-start | bytes 3145732
  35.8 4.4 %copy-start.12 = (f32[4,32,2,1024]{3,2,1,0:T(2,128)S(1)}, f32[4,32,2,1024]{3,2,1,0:T(2,128)}, u32[]{:S(2)}) copy-start(f32[4,32,2,1024]{3,2,1,0:T(2,128)} %param.14) | copy-start | bytes 3145732
  41.4 49.6 %copy-start.29 = (s32[1024]{0:T(1024)S(1)}, s32[1024]{0:T(1024)}, u32[]{:S(2)}) copy-start(s32[1024]{0:T(1024)} %param.17) | copy-start | bytes 12292
  41.5 58.7 %copy-start.35 = (s32[4,2,2]{0,2,1:T(2,128)S(1)}, s32[4,2,2]{0,2,1:T(2,128)}, u32[]{:S(2)}) copy-start(s32[4,2,2]{0,2,1:T(2,128)} %param.15) | copy-start | bytes 196
  41.5 60.0 %copy-start.28 = (f32[4,32,2]{1,0,2:T(4,128)S(1)}, f32[4,32,2]{1,0,2:T(4,128)}, u32[]{:S(2)}) copy-start(f32[4,32,2]{1,0,2:T(4,128)} %get-tuple-element.182) | copy-start | bytes 3076
  120.9 4.4 %copy-start.24 = (f32[1,32,2,1024]{3,1,2,0:T(8,128)S(1)}, f32[1,32,2,1024]{3,1,2,0:T(8,128)}, u32[]{:S(2)}) copy-start(f32[1,32,2,1024]{3,1,2,0:T(8,128)} %get-tuple-element.170) | copy-start | bytes 786436
  120.9 4.4 %copy-start.25 = (f32[1,32,2,1024]{3,1,2,0:T(8,128)S(1)}, f32[1,32,2,1024]{3,1,2,0:T(8,128)}, u32[]{:S(2)}) copy-start(f32[1,32,2,1024]{3,1,2,0:T(8,128)} %get-tuple-element.197) | copy-start | bytes 786436
  129.7 9.3 %copy-start.6 = (f32[4,32,2,1024]{3,1,2,0:T(8,128)}, f32[4,32,2,1024]{3,1,2,0:T(8,128)S(1)}, u32[]{:S(2)}) copy-start(f32[4,32,2,1024]{3,1,2,0:T(8,128)S(1)} %pad.71) | copy-start | bytes 3145732
  129.7 6.9 %copy-start.21 = (f32[2,32,2,1024]{3,1,2,0:T(8,128)S(1)}, f32[2,32,2,1024]{3,1,2,0:T(8,128)}, u32[]{:S(2)}) copy-start(f32[2,32,2,1024]{3,1,2,0:T(8,128)} %get-tuple-element.282) | copy-start | bytes 1572868
  147.9 15.2 %collective-permute-start = (f32[32,2,1024]{2,1,0:T(2,128)S(1)}, f32[32,2,1024]{2,1,0:T(2,128)S(1)}, u32[]{:S(2)}, u32[]{:S(2)}) collective-permute-start(f32[32,2,1024]{2,1,0:T(2,128)S(1)} %bitcast.96), channel_id=1, source_target_pairs={{0,4},{4,8},{8,12},{12,16},{16,20},{20,24},{24,28},{1,5},{5,9},{9,... | collective-permute-start | bytes 786440 | tf_op jit(solution)/shard_map/while/body/eval_jaxpr/ppermute | solution.py:22
  151.5 11.6 %collective-permute-start.1 = (f32[32,2,1024]{2,1,0:T(2,128)S(1)}, f32[32,2,1024]{2,1,0:T(2,128)S(1)}, u32[]{:S(2)}, u32[]{:S(2)}) collective-permute-start(f32[32,2,1024]{2,1,0:T(2,128)S(1)} %bitcast.97), channel_id=1, source_target_pairs={{4,0},{8,4},{12,8},{16,12},{20,16},{24,20},{28,24},{5,1},{9,5},{13... | collective-permute-start | bytes 786440 | tf_op jit(solution)/shard_map/while/body/eval_jaxpr/ppermute | solution.py:22
  163.1 9.8 %collective-permute-start = (f32[32,2,1024]{2,1,0:T(2,128)S(1)}, f32[32,2,1024]{2,1,0:T(2,128)S(1)}, u32[]{:S(2)}, u32[]{:S(2)}) collective-permute-start(f32[32,2,1024]{2,1,0:T(2,128)S(1)} %bitcast.96), channel_id=1, source_target_pairs={{0,4},{4,8},{8,12},{12,16},{16,20},{20,24},{24,28},{1,5},{5,9},{9,... | collective-permute-start | bytes 786440 | tf_op jit(solution)/shard_map/while/body/eval_jaxpr/ppermute | solution.py:22
  167.6 10.6 %collective-permute-start.1 = (f32[32,2,1024]{2,1,0:T(2,128)S(1)}, f32[32,2,1024]{2,1,0:T(2,128)S(1)}, u32[]{:S(2)}, u32[]{:S(2)}) collective-permute-start(f32[32,2,1024]{2,1,0:T(2,128)S(1)} %bitcast.97), channel_id=1, source_target_pairs={{4,0},{8,4},{12,8},{16,12},{20,16},{24,20},{28,24},{5,1},{9,5},{13... | collective-permute-start | bytes 786440 | tf_op jit(solution)/shard_map/while/body/eval_jaxpr/ppermute | solution.py:22
  178.2 9.2 %collective-permute-start = (f32[32,2,1024]{2,1,0:T(2,128)S(1)}, f32[32,2,1024]{2,1,0:T(2,128)S(1)}, u32[]{:S(2)}, u32[]{:S(2)}) collective-permute-start(f32[32,2,1024]{2,1,0:T(2,128)S(1)} %bitcast.96), channel_id=1, source_target_pairs={{0,4},{4,8},{8,12},{12,16},{16,20},{20,24},{24,28},{1,5},{5,9},{9,... | collective-permute-start | bytes 786440 | tf_op jit(solution)/shard_map/while/body/eval_jaxpr/ppermute | solution.py:22
  182.9 11.9 %collective-permute-start.1 = (f32[32,2,1024]{2,1,0:T(2,128)S(1)}, f32[32,2,1024]{2,1,0:T(2,128)S(1)}, u32[]{:S(2)}, u32[]{:S(2)}) collective-permute-start(f32[32,2,1024]{2,1,0:T(2,128)S(1)} %bitcast.97), channel_id=1, source_target_pairs={{4,0},{8,4},{12,8},{16,12},{20,16},{24,20},{28,24},{5,1},{9,5},{13... | collective-permute-start | bytes 786440 | tf_op jit(solution)/shard_map/while/body/eval_jaxpr/ppermute | solution.py:22
  194.9 9.1 %collective-permute-start = (f32[32,2,1024]{2,1,0:T(2,128)S(1)}, f32[32,2,1024]{2,1,0:T(2,128)S(1)}, u32[]{:S(2)}, u32[]{:S(2)}) collective-permute-start(f32[32,2,1024]{2,1,0:T(2,128)S(1)} %bitcast.96), channel_id=1, source_target_pairs={{0,4},{4,8},{8,12},{12,16},{16,20},{20,24},{24,28},{1,5},{5,9},{9,... | collective-permute-start | bytes 786440 | tf_op jit(solution)/shard_map/while/body/eval_jaxpr/ppermute | solution.py:22
  199.5 12.0 %collective-permute-start.1 = (f32[32,2,1024]{2,1,0:T(2,128)S(1)}, f32[32,2,1024]{2,1,0:T(2,128)S(1)}, u32[]{:S(2)}, u32[]{:S(2)}) collective-permute-start(f32[32,2,1024]{2,1,0:T(2,128)S(1)} %bitcast.97), channel_id=1, source_target_pairs={{4,0},{8,4},{12,8},{16,12},{20,16},{24,20},{28,24},{5,1},{9,5},{13... | collective-permute-start | bytes 786440 | tf_op jit(solution)/shard_map/while/body/eval_jaxpr/ppermute | solution.py:22
  211.6 9.1 %collective-permute-start = (f32[32,2,1024]{2,1,0:T(2,128)S(1)}, f32[32,2,1024]{2,1,0:T(2,128)S(1)}, u32[]{:S(2)}, u32[]{:S(2)}) collective-permute-start(f32[32,2,1024]{2,1,0:T(2,128)S(1)} %bitcast.96), channel_id=1, source_target_pairs={{0,4},{4,8},{8,12},{12,16},{16,20},{20,24},{24,28},{1,5},{5,9},{9,... | collective-permute-start | bytes 786440 | tf_op jit(solution)/shard_map/while/body/eval_jaxpr/ppermute | solution.py:22
  216.2 12.0 %collective-permute-start.1 = (f32[32,2,1024]{2,1,0:T(2,128)S(1)}, f32[32,2,1024]{2,1,0:T(2,128)S(1)}, u32[]{:S(2)}, u32[]{:S(2)}) collective-permute-start(f32[32,2,1024]{2,1,0:T(2,128)S(1)} %bitcast.97), channel_id=1, source_target_pairs={{4,0},{8,4},{12,8},{16,12},{20,16},{24,20},{28,24},{5,1},{9,5},{13... | collective-permute-start | bytes 786440 | tf_op jit(solution)/shard_map/while/body/eval_jaxpr/ppermute | solution.py:22
  228.3 9.1 %collective-permute-start = (f32[32,2,1024]{2,1,0:T(2,128)S(1)}, f32[32,2,1024]{2,1,0:T(2,128)S(1)}, u32[]{:S(2)}, u32[]{:S(2)}) collective-permute-start(f32[32,2,1024]{2,1,0:T(2,128)S(1)} %bitcast.96), channel_id=1, source_target_pairs={{0,4},{4,8},{8,12},{12,16},{16,20},{20,24},{24,28},{1,5},{5,9},{9,... | collective-permute-start | bytes 786440 | tf_op jit(solution)/shard_map/while/body/eval_jaxpr/ppermute | solution.py:22
  232.9 12.0 %collective-permute-start.1 = (f32[32,2,1024]{2,1,0:T(2,128)S(1)}, f32[32,2,1024]{2,1,0:T(2,128)S(1)}, u32[]{:S(2)}, u32[]{:S(2)}) collective-permute-start(f32[32,2,1024]{2,1,0:T(2,128)S(1)} %bitcast.97), channel_id=1, source_target_pairs={{4,0},{8,4},{12,8},{16,12},{20,16},{24,20},{28,24},{5,1},{9,5},{13... | collective-permute-start | bytes 786440 | tf_op jit(solution)/shard_map/while/body/eval_jaxpr/ppermute | solution.py:22
  244.9 9.1 %collective-permute-start = (f32[32,2,1024]{2,1,0:T(2,128)S(1)}, f32[32,2,1024]{2,1,0:T(2,128)S(1)}, u32[]{:S(2)}, u32[]{:S(2)}) collective-permute-start(f32[32,2,1024]{2,1,0:T(2,128)S(1)} %bitcast.96), channel_id=1, source_target_pairs={{0,4},{4,8},{8,12},{12,16},{16,20},{20,24},{24,28},{1,5},{5,9},{9,... | collective-permute-start | bytes 786440 | tf_op jit(solution)/shard_map/while/body/eval_jaxpr/ppermute | solution.py:22
  249.6 12.0 %collective-permute-start.1 = (f32[32,2,1024]{2,1,0:T(2,128)S(1)}, f32[32,2,1024]{2,1,0:T(2,128)S(1)}, u32[]{:S(2)}, u32[]{:S(2)}) collective-permute-start(f32[32,2,1024]{2,1,0:T(2,128)S(1)} %bitcast.97), channel_id=1, source_target_pairs={{4,0},{8,4},{12,8},{16,12},{20,16},{24,20},{28,24},{5,1},{9,5},{13... | collective-permute-start | bytes 786440 | tf_op jit(solution)/shard_map/while/body/eval_jaxpr/ppermute | solution.py:22
  (26 other events, 68.1 us)
where the time goes:
time: 271 us; the launch traced here: 267 us
  waiting for transfers between devices  73.1 us (27%)
  blocking collectives  62.2 us (23%)
  local copies, waits for them, and re-layouts  57 us (21%)
  starting transfers between devices  39.8 us (15%)
  other arithmetic  33.2 us (12%)
    ppermute x14, waiting for transfers between devices, passed_along(): return lax.ppermute(x, axis, pairs)  73.1 us
    all_gather x1, blocking collectives, shards(): gathered = lax.all_gather(wall_rows, 'vel', axis=3, tiled=True)  49.5 us
    ppermute x14, starting transfers between devices, passed_along(): return lax.ppermute(x, axis, pairs)  39.8 us
    psum x1, blocking collectives, shards(): lax.psum(velocity_sums(raw_table, flat, integration_coefficient), 'vel')  12.7 us
    pad x4, local copies, waits for them, and re-layouts, shards(): down_a, down_b = lax.associative_scan(compose, (down_a, down_b), axis=0)  12.7 us
    gather x2, local copies, waits for them, and re-layouts, shards(): mirrored = jnp.take(gathered, mirror_slot, axis=3)  8.99 us
    pad x4, local copies, waits for them, and re-layouts, shards(): lax.associative_scan(compose, (jnp.flip(up_a, 0), jnp.flip(up_b, 0)), axi...  6.67 us
  transfers between devices with their start and end apart: 14, of which 13 were waited for; matrix products, arithmetic and copies ran while one was open for 0% of the time, Pallas kernels for 0%

commit v1 on v0

v1 whole, which is shorter than its diff:
```python
import functools
import math

import jax
import jax.numpy as jnp
from jax import lax
from jax.experimental import pallas as pl
from jax.experimental.pallas import tpu as pltpu
from jax.sharding import PartitionSpec as P

VS = 16
LANE = 128
FEAT = 8
MOM = 16
MESH = pl.DeviceIdType.MESH

stream_x = 40.0
stream_y = 0.15
stream_z = 0.05
relaxation_multiplier = 0.05
shear_power_index = 0.81
diffusivity_ratio = 2.0 / 3.0

F32 = jnp.float32
BF16 = jnp.bfloat16


def rounded(x):
    return x.astype(BF16).astype(F32)


def velocity_rows(points):
    spacing = 8.0 / VS
    half = (VS - 1) / 2.0
    bits = VS.bit_length() - 1
    first = lax.shift_right_logical(points, 2 * bits).astype(F32)
    second = (lax.shift_right_logical(points, bits) & (VS - 1)).astype(F32)
    third = (points & (VS - 1)).astype(F32)
    return [(v - half) * spacing for v in (first, second, third)]


def stacked(rows, height):
    index = lax.broadcasted_iota(jnp.int32, (height, LANE), 0)
    out = jnp.zeros((height, LANE), F32)
    for k, row in enumerate(rows):
        out = jnp.where(index == k, row, out)
    return out


def kernel(
    dims,
    wall_mask,
    grid_ref,
    mirror_ref,
    f_hbm,
    out_ref,
    f_ref,
    wall_ref,
    whi_ref,
    wlo_ref,
    mirrored_ref,
    fhi_ref,
    flo_ref,
    tmom_ref,
    gmat_ref,
    mom_ref,
    coef_ref,
    lhs_ref,
    rate_ref,
    prate_ref,
    rate_send,
    rate_recv,
    sa_ref,
    sb_ref,
    pb_ref,
    pair_a,
    pair_b,
    ed_ref,
    eu_ref,
    od_ref,
    ou_ref,
    enter_own,
    enter_send,
    enter_recv,
    f_sem,
    wall_ssem,
    wall_rsem,
    mom_ssem,
    mom_rsem,
    rate_sem,
    face_ssem,
    face_rsem,
    dn_ssem,
    dn_rsem,
    up_ssem,
    up_rsem,
    ret_ssem,
    ret_rsem,
):
    depth, rows, planes, blocks, nspace, nvel = dims
    stride = blocks * planes
    pad = stride
    cells_x = planes * rows
    cells = depth * cells_x
    walls = depth * 2 * planes
    half_blocks = blocks // 2
    pairs = nspace // 2
    weight = (8.0 / VS) ** 3

    s = lax.axis_index("space")
    v = lax.axis_index("vel")
    q = lax.rem(s, 2)
    p = lax.div(s, 2)
    partner = s + 1 - 2 * q
    own0 = q * half_blocks
    far0 = (1 - q) * half_blocks

    def frow(x, y, j, z):
        return pad + (x * rows + y) * stride + j * planes + z

    load = pltpu.make_async_copy(f_hbm, f_ref.at[pl.ds(pad, depth * rows * stride)], f_sem)
    load.start()

    barrier = pltpu.get_barrier_semaphore()
    for d in range(1, nvel):
        pl.semaphore_signal(
            barrier, inc=1, device_id=(s, lax.rem(v + d, nvel)), device_id_type=MESH
        )
    pl.semaphore_signal(barrier, inc=1, device_id=(partner, v), device_id_type=MESH)

    @pl.when(p > 0)
    def _():
        pl.semaphore_signal(barrier, inc=1, device_id=(s - 2, v), device_id_type=MESH)

    @pl.when(p < pairs - 1)
    def _():
        pl.semaphore_signal(barrier, inc=1, device_id=(s + 2, v), device_id_type=MESH)

    tmom_ref[...] = jnp.zeros_like(tmom_ref)
    gmat_ref[...] = jnp.zeros_like(gmat_ref)
    coef_ref[...] = jnp.zeros_like(coef_ref)
    f_ref[pl.ds(0, pad)] = jnp.zeros((pad, LANE), F32)
    f_ref[pl.ds(pad + depth * rows * stride, pad)] = jnp.zeros((pad, LANE), F32)
    for j in range(blocks):
        x1, x2, x3 = velocity_rows(grid_ref[j : j + 1, :])
        one = jnp.ones_like(x1)
        square = x1 * x1 + x2 * x2 + x3 * x3
        cubic = [x * square for x in (x1, x2, x3)]
        cubic_hi = [rounded(x) for x in cubic]
        cubic_lo = [x - h for x, h in zip(cubic, cubic_hi)]
        table = [one, x1, x2, x3, x1 * x1, x2 * x2, x3 * x3, x1 * x2, x1 * x3, x2 * x3]
        tmom_ref[0:MOM, j * LANE : (j + 1) * LANE] = stacked(
            table + cubic_hi + cubic_lo, MOM
        ).astype(BF16)
        feat = stacked(table[:7], FEAT)
        zero = jnp.zeros_like(feat)
        for g in range(3):
            column = [zero] * 9
            for part in range(3):
                column[3 * part + g] = feat
            column = column + [zero]
            gmat_ref[j, 0 : 10 * FEAT, g * LANE : (g + 1) * LANE] = jnp.concatenate(
                column, axis=0
            ).astype(BF16)

    load.wait()

    for x in range(depth):
        for w in range(2):
            for z in range(planes):
                r = (x * 2 + w) * planes + z
                y = (rows - 1) * w
                wall_ref[v, pl.ds(r, blocks, stride=walls), :] = f_ref[
                    pl.ds(frow(x, y, 0, z), blocks, stride=planes), :
                ]

    greetings = nvel + (p > 0).astype(jnp.int32) + (p < pairs - 1).astype(jnp.int32)
    pl.semaphore_wait(barrier, greetings)

    def wall_copy(d):
        return pltpu.make_async_remote_copy(
            src_ref=wall_ref.at[v],
            dst_ref=wall_ref.at[v],
            send_sem=wall_ssem.at[d - 1],
            recv_sem=wall_rsem.at[d - 1],
            device_id=(s, lax.rem(v + d, nvel)),
            device_id_type=MESH,
        )

    def wall_arrival(d):
        origin = lax.rem(v + nvel - d, nvel)
        return pltpu.make_async_remote_copy(
            src_ref=wall_ref.at[origin],
            dst_ref=wall_ref.at[origin],
            send_sem=wall_ssem.at[d - 1],
            recv_sem=wall_rsem.at[d - 1],
            device_id=(s, lax.rem(v + d, nvel)),
            device_id_type=MESH,
        )

    def mom_copy(d):
        return pltpu.make_async_remote_copy(
            src_ref=mom_ref.at[0],
            dst_ref=mom_ref.at[d],
            send_sem=mom_ssem.at[d - 1],
            recv_sem=mom_rsem.at[d - 1],
            device_id=(s, lax.rem(v + d, nvel)),
            device_id_type=MESH,
        )

    for d in range(1, nvel):
        wall_copy(d).start()

    for x in range(depth):
        for z in range(planes):
            base = (x * planes + z) * rows
            for j in range(blocks):
                part = f_ref[pl.ds(frow(x, 0, j, z), rows, stride=stride), :]
                hi = part.astype(BF16)
                lo = (part - hi.astype(F32)).astype(BF16)
                fhi_ref[base : base + rows, j * LANE : (j + 1) * LANE] = hi
                flo_ref[base : base + rows, j * LANE : (j + 1) * LANE] = lo
    contract = (((1,), (1,)), ((), ()))
    sums = lax.dot_general(
        fhi_ref[...], tmom_ref[...], contract, preferred_element_type=F32
    ) + lax.dot_general(flo_ref[...], tmom_ref[...], contract, preferred_element_type=F32)
    mom_ref[0] = sums.T[0:MOM, :]
    for d in range(1, nvel):
        mom_copy(d).start()
    total = mom_ref[0]
    for d in range(1, nvel):
        mom_copy(d).wait_recv()
        total = total + mom_ref[d]
    total = total * weight

    raw = [total[k : k + 1, :] for k in range(MOM)]
    density = raw[0]
    momentum = raw[1:4]
    flow = [m / density for m in momentum]
    tensor = [[raw[4], raw[7], raw[8]], [raw[7], raw[5], raw[9]], [raw[8], raw[9], raw[6]]]
    third = [raw[10 + k] + raw[13 + k] for k in range(3)]
    trace = raw[4] + raw[5] + raw[6]
    flow_sq = flow[0] * flow[0] + flow[1] * flow[1] + flow[2] * flow[2]
    temperature = (trace - density * flow_sq) / (3.0 * density)
    flow_mom = flow[0] * momentum[0] + flow[1] * momentum[1] + flow[2] * momentum[2]
    heat = []
    for k in range(3):
        contracted = flow[0] * tensor[k][0] + flow[1] * tensor[k][1] + flow[2] * tensor[k][2]
        heat.append(
            0.5
            * (
                third[k]
                - 2.0 * contracted
                + flow_sq * momentum[k]
                - flow[k] * trace
                + 2.0 * flow[k] * flow_mom
                - flow[k] * flow_sq * density
            )
        )
    log_t = jnp.log(temperature)
    inverse_t = 1.0 / temperature
    rate = relaxation_multiplier * density * jnp.exp((1.0 - shear_power_index) * log_t)

    rate_send[...] = jnp.broadcast_to(rate, rate_send.shape)

    def rate_copy():
        return pltpu.make_async_remote_copy(
            src_ref=rate_send,
            dst_ref=rate_recv,
            send_sem=rate_sem.at[0],
            recv_sem=rate_sem.at[1],
            device_id=(partner, v),
            device_id_type=MESH,
        )

    rate_copy().start()
    scale = (1.0 - diffusivity_ratio) / 5.0 * inverse_t * inverse_t / density
    flow_heat = flow[0] * heat[0] + flow[1] * heat[1] + flow[2] * heat[2]
    exponent = [
        jnp.log(density) - 1.5 * (log_t + math.log(2.0 * math.pi)) - 0.5 * flow_sq * inverse_t
    ]
    exponent += [u * inverse_t for u in flow] + [-0.5 * inverse_t] * 3
    linear = [-scale * flow_heat] + [scale * h for h in heat]
    bracket = [flow_sq * inverse_t - 5.0]
    bracket += [-2.0 * u * inverse_t for u in flow] + [inverse_t] * 3
    for g, group in enumerate((exponent, linear, bracket)):
        for k, row in enumerate(group):
            coef_ref[g * FEAT + k : g * FEAT + k + 1, :] = row
    whole = coef_ref[0 : 3 * FEAT, :]
    hi = rounded(whole)
    mid = rounded(whole - hi)
    coef_ref[0 : 3 * FEAT, :] = hi
    coef_ref[3 * FEAT : 6 * FEAT, :] = mid
    coef_ref[6 * FEAT : 9 * FEAT, :] = whole - hi - mid
    lhs_ref[...] = coef_ref[...].T.astype(BF16)
    rate_ref[...] = jnp.broadcast_to(rate, (LANE, cells)).T

    for d in range(1, nvel):
        wall_arrival(d).wait_recv()
    everywhere = wall_ref[...].reshape(nvel * blocks * walls, LANE)
    whi = everywhere.astype(BF16)
    whi_ref[...] = whi
    wlo_ref[...] = (everywhere - whi.astype(F32)).astype(BF16)

    def mirror_block(j, carry):
        slot = mirror_ref[pl.ds(j, 1), :]
        low = slot & (LANE - 1)
        high = lax.shift_right_logical(slot, LANE.bit_length() - 1)
        lane_index = lax.broadcasted_iota(jnp.int32, (LANE, LANE), 0)
        pick = jnp.where(lane_index == low, 1.0, 0.0).astype(BF16)
        found = jnp.dot(whi_ref[...], pick, preferred_element_type=F32) + jnp.dot(
            wlo_ref[...], pick, preferred_element_type=F32
        )
        acc = jnp.zeros((walls, LANE), F32)
        for h in range(nvel * blocks):
            acc = acc + jnp.where(high == h, found[h * walls : (h + 1) * walls], 0.0)
        mirrored_ref[j] = acc
        return carry

    lax.fori_loop(0, blocks, mirror_block, 0)

    first_edge = jnp.where(s == 0, 1.0, 0.0).astype(F32)
    last_edge = jnp.where(s == nspace - 1, 1.0, 0.0).astype(F32)
    row_index = lax.broadcasted_iota(jnp.int32, (rows, LANE), 0)

    def block_tables(j):
        return velocity_rows(grid_ref[pl.ds(j, 1), :])

    def local_block(j):
        x1, x2, x3 = block_tables(j)
        pos1 = x1 > 0
        pos2 = x2 > 0
        pos3 = x3 > 0
        coef_y = stream_y * jnp.abs(x2)
        coef_z = stream_z * jnp.abs(x3)
        coef_f = 1.0 - coef_y - coef_z
        sigma = stream_x * jnp.abs(x1)
        opening = 1.0 + sigma
        edge = jnp.where(pos1, first_edge, last_edge)
        mirrored = mirrored_ref[j]
        a_list, b_list, eq_list = [], [], []
        for x in range(depth):
            base = x * cells_x
            got = jnp.dot(
                lhs_ref[base : base + cells_x, :], gmat_ref[j], preferred_element_type=F32
            )
            equilibrium = jnp.exp(got[:, :LANE]) * (
                1.0 + got[:, LANE : 2 * LANE] * got[:, 2 * LANE :]
            )
            rates = rate_ref[base : base + cells_x, :]
            inverse = 1.0 / (opening + rates)
            source = rates * equilibrium
            values = [
                f_ref[pl.ds(frow(x, 0, j, z), rows, stride=stride), :] for z in range(planes)
            ]
            parts = []
            for z in range(planes):
                low = (x * 2) * planes + z
                high = (x * 2 + 1) * planes + z
                mask_low = jnp.full((1, LANE), wall_mask[x, 0, z])
                mask_high = jnp.full((1, LANE), wall_mask[x, 1, z])
                eq_z = equilibrium[z * rows : (z + 1) * rows]
                ghost_low = jnp.where(mask_low == 1, mirrored[low : low + 1], eq_z[0:1])
                ghost_high = jnp.where(
                    mask_high == 1, mirrored[high : high + 1], eq_z[rows - 1 : rows]
                )
                below = f_ref[pl.ds(frow(x, -1, j, z), rows, stride=stride), :]
                above = f_ref[pl.ds(frow(x, 1, j, z), rows, stride=stride), :]
                below = jnp.where(row_index == 0, ghost_low, below)
                above = jnp.where(row_index == rows - 1, ghost_high, above)
                side = jnp.where(pos2, below, above)
                before, after = values[(z - 1) % planes], values[(z + 1) % planes]
                if (z - 1) % planes == (z + 1) % planes:
                    plane = before
                else:
                    plane = jnp.where(pos3, before, after)
                parts.append(coef_f * values[z] + coef_y * side + coef_z * plane)
            b_list.append((jnp.concatenate(parts, axis=0) + source) * inverse)
            a_list.append(sigma * inverse)
            if x in (0, depth - 1):
                eq_list.append(equilibrium)
        a_run = b_run = None
        for k in range(depth):
            a_k = jnp.where(pos1, a_list[k], a_list[depth - 1 - k])
            b_k = jnp.where(pos1, b_list[k], b_list[depth - 1 - k])
            if k == 0:
                target = jnp.where(pos1, eq_list[0], eq_list[-1])
                b_run = b_k + a_k * (edge * target)
                a_run = a_k * (1.0 - edge)
            else:
                b_run = a_k * b_run + b_k
                a_run = a_k * a_run
            sa_ref[j, k] = a_run
            sb_ref[j, k] = b_run

    def face_copy(c):
        return pltpu.make_async_remote_copy(
            src_ref=sb_ref.at[far0 + c, depth - 1],
            dst_ref=pb_ref.at[c],
            send_sem=face_ssem.at[c],
            recv_sem=face_rsem.at[c],
            device_id=(partner, v),
            device_id_type=MESH,
        )

    def far_block(c, carry):
        local_block(far0 + c)
        face_copy(c).start()
        return carry

    def own_block(c, carry):
        local_block(own0 + c)
        return carry

    lax.fori_loop(0, half_blocks, far_block, 0)
    lax.fori_loop(0, half_blocks, own_block, 0)

    rate_copy().wait()
    prate_ref[...] = jnp.broadcast_to(rate_recv[0:1, :], (LANE, cells)).T


    def first_weight(x1):
        sign = jnp.where(x1 > 0, 1.0, -1.0)
        return sign * jnp.where(q == 0, 1.0, -1.0) > 0

    def pair_block(c, carry):
        j = own0 + c
        x1, _, _ = block_tables(j)
        sigma = stream_x * jnp.abs(x1)
        opening = 1.0 + sigma
        other = None
        for x in range(depth):
            a = sigma / (opening + prate_ref[x * cells_x : (x + 1) * cells_x, :])
            other = a if other is None else other * a
        face_copy(c).wait_recv()
        a_own = sa_ref[j, depth - 1]
        b_own = sb_ref[j, depth - 1]
        b_other = pb_ref[c]
        first = first_weight(x1)
        pair_a[c, 0] = other
        pair_a[c, 1] = a_own * other
        pair_b[c] = jnp.where(first, other * b_own + b_other, a_own * b_other + b_own)
        return carry

    lax.fori_loop(0, half_blocks, pair_block, 0)

    def down_copy(c):
        return pltpu.make_async_remote_copy(
            src_ref=od_ref.at[c],
            dst_ref=ed_ref.at[c],
            send_sem=dn_ssem.at[c],
            recv_sem=dn_rsem.at[c],
            device_id=(s + 2, v),
            device_id_type=MESH,
        )

    def up_copy(c):
        return pltpu.make_async_remote_copy(
            src_ref=ou_ref.at[c],
            dst_ref=eu_ref.at[c],
            send_sem=up_ssem.at[c],
            recv_sem=up_rsem.at[c],
            device_id=(s - 2, v),
            device_id_type=MESH,
        )

    def return_copy(c):
        return pltpu.make_async_remote_copy(
            src_ref=enter_send.at[c],
            dst_ref=enter_recv.at[c],
            send_sem=ret_ssem.at[c],
            recv_sem=ret_rsem.at[c],
            device_id=(partner, v),
            device_id_type=MESH,
        )

    @pl.when(p == 0)
    def _():
        ed_ref[...] = jnp.zeros_like(ed_ref)

    @pl.when(p == pairs - 1)
    def _():
        eu_ref[...] = jnp.zeros_like(eu_ref)

    back = pairs - 1 - p
    latest = jnp.maximum(p, back)

    def chain_step(t, carry):
        c_dn = t - p
        c_up = t - back
        c_end = t - latest

        @pl.when((c_dn >= 0) & (c_dn < half_blocks))
        def _():
            @pl.when(p > 0)
            def _():
                down_copy(c_dn).wait_recv()

            @pl.when(p < pairs - 1)
            def _():
                od_ref[c_dn] = pair_a[c_dn, 1] * ed_ref[c_dn] + pair_b[c_dn]
                down_copy(c_dn).start()

        @pl.when((c_up >= 0) & (c_up < half_blocks))
        def _():
            @pl.when(p < pairs - 1)
            def _():
                up_copy(c_up).wait_recv()

            @pl.when(p > 0)
            def _():
                ou_ref[c_up] = pair_a[c_up, 1] * eu_ref[c_up] + pair_b[c_up]
                up_copy(c_up).start()

        @pl.when((c_end >= 0) & (c_end < half_blocks))
        def _():
            j = own0 + c_end
            x1, _, _ = block_tables(j)
            enter = jnp.where(x1 > 0, ed_ref[c_end], eu_ref[c_end])
            first = first_weight(x1)
            after_own = sa_ref[j, depth - 1] * enter + sb_ref[j, depth - 1]
            after_other = pair_a[c_end, 0] * enter + pb_ref[c_end]
            enter_send[c_end] = jnp.where(first, after_own, enter)
            return_copy(c_end).start()
            enter_own[c_end] = jnp.where(first, enter, after_other)

        return carry

    lax.fori_loop(0, half_blocks + pairs - 1, chain_step, 0)

    def finish(j, enter):
        x1, _, _ = block_tables(j)
        pos1 = x1 > 0
        done = [sa_ref[j, k] * enter + sb_ref[j, k] for k in range(depth)]
        for x in range(depth):
            value = jnp.where(pos1, done[x], done[depth - 1 - x])
            for z in range(planes):
                out_ref[pl.ds(frow(x, 0, j, z) - pad, rows, stride=stride), :] = value[
                    z * rows : (z + 1) * rows
                ]

    def finish_own(c, carry):
        finish(own0 + c, enter_own[c])
        return carry

    def finish_far(c, carry):
        return_copy(c).wait_recv()
        finish(far0 + c, enter_recv[c])
        return carry

    lax.fori_loop(0, half_blocks, finish_own, 0)
    lax.fori_loop(0, half_blocks, finish_far, 0)

    for d in range(1, nvel):
        wall_copy(d).wait_send()
        mom_copy(d).wait_send()

    def drain(c, carry):
        face_copy(c).wait_send()
        return_copy(c).wait_send()

        @pl.when(p < pairs - 1)
        def _():
            down_copy(c).wait_send()

        @pl.when(p > 0)
        def _():
            up_copy(c).wait_send()

        return carry

    lax.fori_loop(0, half_blocks, drain, 0)


def shards(nspace, nvel, distribution, wall_mask, grid_point, mirror_slot):
    depth, rows, planes, width = distribution.shape
    blocks = width // LANE
    half = blocks // 2
    dims = (depth, rows, planes, blocks, nspace, nvel)
    count = depth * rows * planes * blocks
    stride = blocks * planes
    side = planes * rows
    cells = depth * side
    walls = depth * 2 * planes
    flat = (
        distribution.reshape(depth, rows, planes, blocks, LANE)
        .transpose(0, 1, 3, 2, 4)
        .reshape(count, LANE)
    )
    vmem = pl.BlockSpec(memory_space=pltpu.VMEM)
    face = (half, side, LANE)
    out = pl.pallas_call(
        functools.partial(kernel, dims),
        out_shape=jax.ShapeDtypeStruct((count, LANE), F32),
        in_specs=[
            pl.BlockSpec(memory_space=pltpu.SMEM),
            vmem,
            vmem,
            pl.BlockSpec(memory_space=pl.ANY),
        ],
        out_specs=vmem,
        scratch_shapes=[
            pltpu.VMEM((count + 2 * stride, LANE), F32),
            pltpu.VMEM((nvel, blocks * walls, LANE), F32),
            pltpu.VMEM((nvel * blocks * walls, LANE), BF16),
            pltpu.VMEM((nvel * blocks * walls, LANE), BF16),
            pltpu.VMEM((blocks, walls, LANE), F32),
            pltpu.VMEM((cells, width), BF16),
            pltpu.VMEM((cells, width), BF16),
            pltpu.VMEM((LANE, width), BF16),
            pltpu.VMEM((blocks, LANE, 3 * LANE), BF16),
            pltpu.VMEM((nvel, MOM, cells), F32),
            pltpu.VMEM((LANE, cells), F32),
            pltpu.VMEM((cells, LANE), BF16),
            pltpu.VMEM((cells, LANE), F32),
            pltpu.VMEM((cells, LANE), F32),
            pltpu.VMEM((8, cells), F32),
            pltpu.VMEM((8, cells), F32),
            pltpu.VMEM((blocks, depth, side, LANE), F32),
            pltpu.VMEM((blocks, depth, side, LANE), F32),
            pltpu.VMEM(face, F32),
            pltpu.VMEM((half, 2, side, LANE), F32),
            pltpu.VMEM(face, F32),
            pltpu.VMEM(face, F32),
            pltpu.VMEM(face, F32),
            pltpu.VMEM(face, F32),
            pltpu.VMEM(face, F32),
            pltpu.VMEM(face, F32),
            pltpu.VMEM(face, F32),
            pltpu.VMEM(face, F32),
            pltpu.SemaphoreType.DMA,
            pltpu.SemaphoreType.DMA((nvel - 1,)),
            pltpu.SemaphoreType.DMA((nvel - 1,)),
            pltpu.SemaphoreType.DMA((nvel - 1,)),
            pltpu.SemaphoreType.DMA((nvel - 1,)),
            pltpu.SemaphoreType.DMA((2,)),
        ]
        + [pltpu.SemaphoreType.DMA((half,))] * 8,
        compiler_params=pltpu.CompilerParams(
            collective_id=0, has_side_effects=True, vmem_limit_bytes=40 * 1024 * 1024
        ),
    )(wall_mask, grid_point.reshape(blocks, LANE), mirror_slot.reshape(blocks, LANE), flat)
    return (
        out.reshape(depth, rows, blocks, planes, LANE)
        .transpose(0, 1, 3, 2, 4)
        .reshape(depth, rows, planes, width)
    )


def solution(mesh):
    placed = (P("space", None, None, "vel"), P("space", None, None), P("vel"), P("vel"))
    body = functools.partial(shards, mesh.shape["space"], mesh.shape["vel"])
    return jax.shard_map(
        body, mesh=mesh, in_specs=placed, out_specs=P("space", None, None, "vel"), check_vma=False
    )
```

time: 271 us -> 40.5 us (0.15); the launches traced: 267 us -> 40.3 us
  waiting for transfers between devices: 73.1 us -> 0 us
  blocking collectives: 62.2 us -> 0 us
  local copies, waits for them, and re-layouts: 57 us -> 2.98 us
  starting transfers between devices: 39.8 us -> 0 us
  Pallas kernels: 0 us -> 37.3 us
  other arithmetic: 33.2 us -> 0 us
    ppermute x14 -> x0, waiting for transfers between devices: 73.1 us -> none  [passed_along(): return lax.ppermute(x, axis, pairs)]
    all_gather x1 -> x0, blocking collectives: 49.5 us -> none  [shards(): gathered = lax.all_gather(wall_rows, 'vel', axis=3, tiled=True)]
    ppermute x14 -> x0, starting transfers between devices: 39.8 us -> none  [passed_along(): return lax.ppermute(x, axis, pairs)]
    pallas_call x0 -> x1, Pallas kernels: none -> 37.3 us  [shards(): pl.pallas_call(functools.partial(kernel, dims), out_shape=jax.ShapeDtypeS...]
    pad x8 -> x0, local copies, waits for them, and re-layouts: 19.4 us -> none  [the longest x4 12.7 us: shards(): down_a, down_b = lax.associative_scan(compose, (down_a, down_b), axis=0)]
    squeeze x37 -> x0, local copies, waits for them, and re-layouts: 12.8 us -> none  [the longest x1 2.83 us: shards(): peculiar[1] * heat[1][:, None]]
    psum x1 -> x0, blocking collectives: 12.7 us -> none  [shards(): lax.psum(velocity_sums(raw_table, flat, integration_coefficient), 'vel')]
    mul x9 -> x0, other arithmetic: 11.8 us -> none  [the longest x4 5.4 us: compose(): return (later[0] * earlier[0], later[0] * earlier[1] + later[1])]
  transfers between devices with their start and end apart: 14 -> 0, of which waited for: 13 -> 0; matrix products, arithmetic and copies ran while one was open for 0% -> 0% of each run, Pallas kernels for 0% -> 0%
where the time goes in v1:
time: 40.5 us; the launch traced here: 40.3 us
  Pallas kernels  37.3 us (92%)
  local copies, waits for them, and re-layouts  2.98 us (7%)
    pallas_call x1, Pallas kernels, shards(): pl.pallas_call(functools.partial(kernel, dims), out_shape=jax.ShapeDtypeS...  37.3 us
    unnamed x10, local copies, waits for them, and re-layouts  2.98 us

profile of v1, /device:TPU:0, one launch (start us, length us, event | category | flops | bytes accessed | tf_op | source)
XLA Modules:
  0.0 40.3 jit_solution(12692947201413607241)
XLA Ops:
  0.0 0.0 copy-start.3
  0.0 0.0 copy-start.2
  0.0 0.0 copy-start.1
  0.0 0.7 %copy-done.3 = s32[4,2,2]{0,2,1:T(2,128)S(1)} copy-done((s32[4,2,2]{0,2,1:T(2,128)S(1)}, s32[4,2,2]{0,2,1:T(2,128)}, u32[]{:S(2)}) %copy-start.3) | copy-done | bytes 88
  0.7 0.1 copy.6.wall_mask
  0.8 0.0 copy-done.2
  0.8 0.0 copy-done.1
  0.8 0.0 copy-start
  0.8 1.2 %copy-done = f32[4,32,2,1024]{3,2,1,0:T(2,128)S(1)} copy-done((f32[4,32,2,1024]{3,2,1,0:T(2,128)S(1)}, f32[4,32,2,1024]{3,2,1,0:T(2,128)}, u32[]{:S(2)}) %copy-start) | copy-done | bytes 1048600
  2.0 37.3 %shard_map.46 = f32[2048,128]{1,0:T(8,128)S(1)} custom-call(s32[4,2,2]{2,1,0:T(2,128)S(1)} %copy.6.wall_mask, s32[8,128]{1,0:T(8,128)S(1)} %bitcast.14, s32[8,128]{1,0:T(8,128)S(1)} %bitcast.15, f32[2048,128]{1,0:T(8,128)S(1)} %bitcast.13), custom_call_target="tpu_custom_call" | custom-call | tf_op jit(solution)/shard_map/pallas_call | solution.py:592
  39.3 1.0 %copy.9 = f32[4,32,2,1024]{3,2,1,0:T(2,128)} copy(f32[4,32,2,1024]{3,2,1,0:T(2,128)S(1)} %bitcast.12) | data formatting | bytes 2097152
Async XLA Ops:
  0.0 0.7 %copy-start.3 = (s32[4,2,2]{0,2,1:T(2,128)S(1)}, s32[4,2,2]{0,2,1:T(2,128)}, u32[]{:S(2)}) copy-start(s32[4,2,2]{0,2,1:T(2,128)} %param.5) | copy-start | bytes 196
  0.0 0.8 %copy-start.2 = (s32[1024]{0:T(1024)S(1)}, s32[1024]{0:T(1024)}, u32[]{:S(2)}) copy-start(s32[1024]{0:T(1024)} %param.7) | copy-start | bytes 12292
  0.0 0.8 %copy-start.1 = (s32[1024]{0:T(1024)S(1)}, s32[1024]{0:T(1024)}, u32[]{:S(2)}) copy-start(s32[1024]{0:T(1024)} %param.6) | copy-start | bytes 12292
  0.8 1.2 %copy-start = (f32[4,32,2,1024]{3,2,1,0:T(2,128)S(1)}, f32[4,32,2,1024]{3,2,1,0:T(2,128)}, u32[]{:S(2)}) copy-start(f32[4,32,2,1024]{3,2,1,0:T(2,128)} %param.4) | copy-start | bytes 3145732

commit v2 on v1

--- a/solution.py
+++ b/solution.py
@@ -56,8 +56,10 @@
     out_ref,
     f_ref,
     wall_ref,
-    whi_ref,
-    wlo_ref,
+    wsplit_ref,
+    pick_ref,
+    cell_ref,
+    eq_ref,
     mirrored_ref,
     fhi_ref,
     flo_ref,
@@ -99,7 +101,6 @@
 ):
     depth, rows, planes, blocks, nspace, nvel = dims
     stride = blocks * planes
-    pad = stride
     cells_x = planes * rows
     cells = depth * cells_x
     walls = depth * 2 * planes
@@ -116,9 +117,9 @@
     far0 = (1 - q) * half_blocks
 
     def frow(x, y, j, z):
-        return pad + (x * rows + y) * stride + j * planes + z
-
-    load = pltpu.make_async_copy(f_hbm, f_ref.at[pl.ds(pad, depth * rows * stride)], f_sem)
+        return (x * rows + y) * stride + j * planes + z
+
+    load = pltpu.make_async_copy(f_hbm, f_ref, f_sem)
     load.start()
 
     barrier = pltpu.get_barrier_semaphore()
@@ -139,8 +140,6 @@
     tmom_ref[...] = jnp.zeros_like(tmom_ref)
     gmat_ref[...] = jnp.zeros_like(gmat_ref)
     coef_ref[...] = jnp.zeros_like(coef_ref)
-    f_ref[pl.ds(0, pad)] = jnp.zeros((pad, LANE), F32)
-    f_ref[pl.ds(pad + depth * rows * stride, pad)] = jnp.zeros((pad, LANE), F32)
     for j in range(blocks):
         x1, x2, x3 = velocity_rows(grid_ref[j : j + 1, :])
         one = jnp.ones_like(x1)
@@ -163,6 +162,10 @@
                 column, axis=0
             ).astype(BF16)
 
+        slot = mirror_ref[j : j + 1, :]
+        index = lax.broadcasted_iota(jnp.int32, (2 * LANE, LANE), 0) & (LANE - 1)
+        pick_ref[j] = jnp.where(index == (slot & (LANE - 1)), 1.0, 0.0).astype(BF16)
+
     load.wait()
 
     for x in range(depth):
@@ -177,39 +180,48 @@
     greetings = nvel + (p > 0).astype(jnp.int32) + (p < pairs - 1).astype(jnp.int32)
     pl.semaphore_wait(barrier, greetings)
 
-    def wall_copy(d):
-        return pltpu.make_async_remote_copy(
-            src_ref=wall_ref.at[v],
-            dst_ref=wall_ref.at[v],
-            send_sem=wall_ssem.at[d - 1],
-            recv_sem=wall_rsem.at[d - 1],
-            device_id=(s, lax.rem(v + d, nvel)),
-            device_id_type=MESH,
-        )
-
-    def wall_arrival(d):
-        origin = lax.rem(v + nvel - d, nvel)
+    sibling = v + 1 - 2 * lax.rem(v, 2)
+    twins = nvel // 2
+
+    def far(base, m):
+        return lax.rem(base + 2 * m + nvel, nvel)
+
+    def wall_copy(k, origin, target):
         return pltpu.make_async_remote_copy(
             src_ref=wall_ref.at[origin],
             dst_ref=wall_ref.at[origin],
-            send_sem=wall_ssem.at[d - 1],
-            recv_sem=wall_rsem.at[d - 1],
-            device_id=(s, lax.rem(v + d, nvel)),
+            send_sem=wall_ssem.at[k],
+            recv_sem=wall_rsem.at[k],
+            device_id=(s, target),
             device_id_type=MESH,
         )
 
-    def mom_copy(d):
+    def wall_far(m):
+        return wall_copy(m, v, far(v, m))
+
+    def wall_far_arrival(m):
+        return wall_copy(m, far(v, -m), far(v, m))
+
+    def wall_forward(m):
+        return wall_copy(twins - 1 + m, far(v, -m), sibling)
+
+    def wall_forward_arrival(m):
+        return wall_copy(twins - 1 + m, far(sibling, -m), sibling)
+
+    def mom_copy(k):
+        target = far(v if k % 2 == 0 else sibling, k // 2)
         return pltpu.make_async_remote_copy(
             src_ref=mom_ref.at[0],
-            dst_ref=mom_ref.at[d],
-            send_sem=mom_ssem.at[d - 1],
-            recv_sem=mom_rsem.at[d - 1],
-            device_id=(s, lax.rem(v + d, nvel)),
+            dst_ref=mom_ref.at[k],
+            send_sem=mom_ssem.at[k - 1],
+            recv_sem=mom_rsem.at[k - 1],
+            device_id=(s, target),
             device_id_type=MESH,
         )
 
-    for d in range(1, nvel):
-        wall_copy(d).start()
+    for m in range(1, twins):
+        wall_far(m).start()
+    wall_copy(0, v, sibling).start()
 
     for x in range(depth):
         for z in range(planes):
@@ -218,6 +230,7 @@
                 part = f_ref[pl.ds(frow(x, 0, j, z), rows, stride=stride), :]
                 hi = part.astype(BF16)
                 lo = (part - hi.astype(F32)).astype(BF16)
+                cell_ref[j, x, z * rows : (z + 1) * rows, :] = part
                 fhi_ref[base : base + rows, j * LANE : (j + 1) * LANE] = hi
                 flo_ref[base : base + rows, j * LANE : (j + 1) * LANE] = lo
     contract = (((1,), (1,)), ((), ()))
@@ -225,8 +238,11 @@
         fhi_ref[...], tmom_ref[...], contract, preferred_element_type=F32
     ) + lax.dot_general(flo_ref[...], tmom_ref[...], contract, preferred_element_type=F32)
     mom_ref[0] = sums.T[0:MOM, :]
-    for d in range(1, nvel):
+    for d in range(nvel - 1, 0, -1):
         mom_copy(d).start()
+    for m in range(1, twins):
+        wall_far_arrival(m).wait_recv()
+        wall_forward(m).start()
     total = mom_ref[0]
     for d in range(1, nvel):
         mom_copy(d).wait_recv()
@@ -295,29 +311,26 @@
     lhs_ref[...] = coef_ref[...].T.astype(BF16)
     rate_ref[...] = jnp.broadcast_to(rate, (LANE, cells)).T
 
-    for d in range(1, nvel):
-        wall_arrival(d).wait_recv()
+    for j in range(blocks):
+        got = jnp.dot(lhs_ref[...], gmat_ref[j], preferred_element_type=F32)
+        eq_ref[j] = jnp.exp(got[:, :LANE]) * (
+            1.0 + got[:, LANE : 2 * LANE] * got[:, 2 * LANE :]
+        )
+
+    wall_copy(0, sibling, sibling).wait_recv()
+    for m in range(1, twins):
+        wall_forward_arrival(m).wait_recv()
     everywhere = wall_ref[...].reshape(nvel * blocks * walls, LANE)
     whi = everywhere.astype(BF16)
-    whi_ref[...] = whi
-    wlo_ref[...] = (everywhere - whi.astype(F32)).astype(BF16)
-
-    def mirror_block(j, carry):
-        slot = mirror_ref[pl.ds(j, 1), :]
-        low = slot & (LANE - 1)
-        high = lax.shift_right_logical(slot, LANE.bit_length() - 1)
-        lane_index = lax.broadcasted_iota(jnp.int32, (LANE, LANE), 0)
-        pick = jnp.where(lane_index == low, 1.0, 0.0).astype(BF16)
-        found = jnp.dot(whi_ref[...], pick, preferred_element_type=F32) + jnp.dot(
-            wlo_ref[...], pick, preferred_element_type=F32
-        )
+    wsplit_ref[:, :LANE] = whi
+    wsplit_ref[:, LANE:] = (everywhere - whi.astype(F32)).astype(BF16)
+    for j in range(blocks):
+        high = lax.shift_right_logical(mirror_ref[j : j + 1, :], LANE.bit_length() - 1)
+        found = jnp.dot(wsplit_ref[...], pick_ref[j], preferred_element_type=F32)
         acc = jnp.zeros((walls, LANE), F32)
         for h in range(nvel * blocks):
             acc = acc + jnp.where(high == h, found[h * walls : (h + 1) * walls], 0.0)
         mirrored_ref[j] = acc
-        return carry
-
-    lax.fori_loop(0, blocks, mirror_block, 0)
 
     first_edge = jnp.where(s == 0, 1.0, 0.0).astype(F32)
     last_edge = jnp.where(s == nspace - 1, 1.0, 0.0).astype(F32)
@@ -341,17 +354,12 @@
         a_list, b_list, eq_list = [], [], []
         for x in range(depth):
             base = x * cells_x
-            got = jnp.dot(
-                lhs_ref[base : base + cells_x, :], gmat_ref[j], preferred_element_type=F32
-            )
-            equilibrium = jnp.exp(got[:, :LANE]) * (
-                1.0 + got[:, LANE : 2 * LANE] * got[:, 2 * LANE :]
-            )
+            equilibrium = eq_ref[j, base : base + cells_x, :]
             rates = rate_ref[base : base + cells_x, :]
             inverse = 1.0 / (opening + rates)
             source = rates * equilibrium
             values = [
-                f_ref[pl.ds(frow(x, 0, j, z), rows, stride=stride), :] for z in range(planes)
+                cell_ref[j, x, z * rows : (z + 1) * rows, :] for z in range(planes)
             ]
             parts = []
             for z in range(planes):
@@ -364,8 +372,8 @@
                 ghost_high = jnp.where(
                     mask_high == 1, mirrored[high : high + 1], eq_z[rows - 1 : rows]
                 )
-                below = f_ref[pl.ds(frow(x, -1, j, z), rows, stride=stride), :]
-                above = f_ref[pl.ds(frow(x, 1, j, z), rows, stride=stride), :]
+                below = pltpu.roll(values[z], 1, axis=0)
+                above = pltpu.roll(values[z], rows - 1, axis=0)
                 below = jnp.where(row_index == 0, ghost_low, below)
                 above = jnp.where(row_index == rows - 1, ghost_high, above)
                 side = jnp.where(pos2, below, above)
@@ -535,7 +543,7 @@
         for x in range(depth):
             value = jnp.where(pos1, done[x], done[depth - 1 - x])
             for z in range(planes):
-                out_ref[pl.ds(frow(x, 0, j, z) - pad, rows, stride=stride), :] = value[
+                out_ref[pl.ds(frow(x, 0, j, z), rows, stride=stride), :] = value[
                     z * rows : (z + 1) * rows
                 ]
 
@@ -551,8 +559,11 @@
     lax.fori_loop(0, half_blocks, finish_own, 0)
     lax.fori_loop(0, half_blocks, finish_far, 0)
 
+    wall_copy(0, v, sibling).wait_send()
+    for m in range(1, twins):
+        wall_far(m).wait_send()
+        wall_forward(m).wait_send()
     for d in range(1, nvel):
-        wall_copy(d).wait_send()
         mom_copy(d).wait_send()
 
     def drain(c, carry):
@@ -600,10 +611,12 @@
         ],
         out_specs=vmem,
         scratch_shapes=[
-            pltpu.VMEM((count + 2 * stride, LANE), F32),
+            pltpu.VMEM((count, LANE), F32),
             pltpu.VMEM((nvel, blocks * walls, LANE), F32),
-            pltpu.VMEM((nvel * blocks * walls, LANE), BF16),
-            pltpu.VMEM((nvel * blocks * walls, LANE), BF16),
+            pltpu.VMEM((nvel * blocks * walls, 2 * LANE), BF16),
+            pltpu.VMEM((blocks, 2 * LANE, LANE), BF16),
+            pltpu.VMEM((blocks, depth, side, LANE), F32),
+            pltpu.VMEM((blocks, cells, LANE), F32),
             pltpu.VMEM((blocks, walls, LANE), F32),
             pltpu.VMEM((cells, width), BF16),
             pltpu.VMEM((cells, width), BF16),

time: 40.5 us -> 38.5 us (0.951)
  Pallas kernels: 37.3 us -> 35.3 us
    pallas_call x1, Pallas kernels: 37.3 us -> 35.3 us  [shards(): pl.pallas_call(functools.partial(kernel, dims), out_shape=jax.ShapeDtypeS...]
where the time goes in v2:
time: 38.5 us; the launch traced here: 38.3 us
  Pallas kernels  35.3 us (92%)
  local copies, waits for them, and re-layouts  2.98 us (8%)
    pallas_call x1, Pallas kernels, shards(): pl.pallas_call(functools.partial(kernel, dims), out_shape=jax.ShapeDtypeS...  35.3 us
    unnamed x10, local copies, waits for them, and re-layouts  2.98 us

profile of v2, /device:TPU:0, one launch (start us, length us, event | category | flops | bytes accessed | tf_op | source)
XLA Modules:
  0.0 38.3 jit_solution(13359013924518327672)
XLA Ops:
  0.0 0.0 copy-start.3
  0.0 0.0 copy-start.2
  0.0 0.0 copy-start.1
  0.0 0.7 %copy-done.3 = s32[4,2,2]{0,2,1:T(2,128)S(1)} copy-done((s32[4,2,2]{0,2,1:T(2,128)S(1)}, s32[4,2,2]{0,2,1:T(2,128)}, u32[]{:S(2)}) %copy-start.3) | copy-done | bytes 88
  0.7 0.1 copy.6.wall_mask
  0.8 0.0 copy-done.2
  0.8 0.0 copy-done.1
  0.8 0.0 copy-start
  0.8 1.2 %copy-done = f32[4,32,2,1024]{3,2,1,0:T(2,128)S(1)} copy-done((f32[4,32,2,1024]{3,2,1,0:T(2,128)S(1)}, f32[4,32,2,1024]{3,2,1,0:T(2,128)}, u32[]{:S(2)}) %copy-start) | copy-done | bytes 1048600
  2.0 35.3 %shard_map.46 = f32[2048,128]{1,0:T(8,128)S(1)} custom-call(s32[4,2,2]{2,1,0:T(2,128)S(1)} %copy.6.wall_mask, s32[8,128]{1,0:T(8,128)S(1)} %bitcast.14, s32[8,128]{1,0:T(8,128)S(1)} %bitcast.15, f32[2048,128]{1,0:T(8,128)S(1)} %bitcast.13), custom_call_target="tpu_custom_call" | custom-call | tf_op jit(solution)/shard_map/pallas_call | solution.py:603
  37.3 1.0 %copy.9 = f32[4,32,2,1024]{3,2,1,0:T(2,128)} copy(f32[4,32,2,1024]{3,2,1,0:T(2,128)S(1)} %bitcast.12) | data formatting | bytes 2097152
Async XLA Ops:
  0.0 0.7 %copy-start.3 = (s32[4,2,2]{0,2,1:T(2,128)S(1)}, s32[4,2,2]{0,2,1:T(2,128)}, u32[]{:S(2)}) copy-start(s32[4,2,2]{0,2,1:T(2,128)} %param.5) | copy-start | bytes 196
  0.0 0.8 %copy-start.2 = (s32[1024]{0:T(1024)S(1)}, s32[1024]{0:T(1024)}, u32[]{:S(2)}) copy-start(s32[1024]{0:T(1024)} %param.7) | copy-start | bytes 12292
  0.0 0.8 %copy-start.1 = (s32[1024]{0:T(1024)S(1)}, s32[1024]{0:T(1024)}, u32[]{:S(2)}) copy-start(s32[1024]{0:T(1024)} %param.6) | copy-start | bytes 12292
  0.8 1.2 %copy-start = (f32[4,32,2,1024]{3,2,1,0:T(2,128)S(1)}, f32[4,32,2,1024]{3,2,1,0:T(2,128)}, u32[]{:S(2)}) copy-start(f32[4,32,2,1024]{3,2,1,0:T(2,128)} %param.4) | copy-start | bytes 3145732

commit v3 on v2

--- a/solution.py
+++ b/solution.py
@@ -243,6 +243,40 @@
     for m in range(1, twins):
         wall_far_arrival(m).wait_recv()
         wall_forward(m).start()
+    row_index = lax.broadcasted_iota(jnp.int32, (rows, LANE), 0)
+
+    def block_tables(j):
+        return velocity_rows(grid_ref[pl.ds(j, 1), :])
+
+    def flux_block(j, carry):
+        _, x2, x3 = block_tables(j)
+        pos2 = x2 > 0
+        pos3 = x3 > 0
+        coef_y = stream_y * jnp.abs(x2)
+        coef_z = stream_z * jnp.abs(x3)
+        coef_f = 1.0 - coef_y - coef_z
+        for x in range(depth):
+            values = [
+                cell_ref[j, x, z * rows : (z + 1) * rows, :] for z in range(planes)
+            ]
+            for z in range(planes):
+                below = jnp.where(row_index == 0, 0.0, pltpu.roll(values[z], 1, axis=0))
+                above = jnp.where(
+                    row_index == rows - 1, 0.0, pltpu.roll(values[z], rows - 1, axis=0)
+                )
+                side = jnp.where(pos2, below, above)
+                before, after = values[(z - 1) % planes], values[(z + 1) % planes]
+                if (z - 1) % planes == (z + 1) % planes:
+                    plane = before
+                else:
+                    plane = jnp.where(pos3, before, after)
+                sb_ref[j, x, z * rows : (z + 1) * rows, :] = (
+                    coef_f * values[z] + coef_y * side + coef_z * plane
+                )
+        return carry
+
+    lax.fori_loop(0, blocks, flux_block, 0)
+
     total = mom_ref[0]
     for d in range(1, nvel):
         mom_copy(d).wait_recv()
@@ -334,56 +368,42 @@
 
     first_edge = jnp.where(s == 0, 1.0, 0.0).astype(F32)
     last_edge = jnp.where(s == nspace - 1, 1.0, 0.0).astype(F32)
-    row_index = lax.broadcasted_iota(jnp.int32, (rows, LANE), 0)
-
-    def block_tables(j):
-        return velocity_rows(grid_ref[pl.ds(j, 1), :])
-
     def local_block(j):
-        x1, x2, x3 = block_tables(j)
+        x1, x2, _ = block_tables(j)
         pos1 = x1 > 0
         pos2 = x2 > 0
-        pos3 = x3 > 0
         coef_y = stream_y * jnp.abs(x2)
-        coef_z = stream_z * jnp.abs(x3)
-        coef_f = 1.0 - coef_y - coef_z
+        coef_low = jnp.where(pos2, coef_y, 0.0)
+        coef_high = jnp.where(pos2, 0.0, coef_y)
         sigma = stream_x * jnp.abs(x1)
         opening = 1.0 + sigma
         edge = jnp.where(pos1, first_edge, last_edge)
         mirrored = mirrored_ref[j]
+        group_index = lax.broadcasted_iota(jnp.int32, (8, LANE), 0)
         a_list, b_list, eq_list = [], [], []
         for x in range(depth):
             base = x * cells_x
             equilibrium = eq_ref[j, base : base + cells_x, :]
             rates = rate_ref[base : base + cells_x, :]
             inverse = 1.0 / (opening + rates)
-            source = rates * equilibrium
-            values = [
-                cell_ref[j, x, z * rows : (z + 1) * rows, :] for z in range(planes)
-            ]
             parts = []
             for z in range(planes):
                 low = (x * 2) * planes + z
                 high = (x * 2 + 1) * planes + z
-                mask_low = jnp.full((1, LANE), wall_mask[x, 0, z])
-                mask_high = jnp.full((1, LANE), wall_mask[x, 1, z])
+                mask_low = jnp.full((1, LANE), wall_mask[0, z, x])
+                mask_high = jnp.full((1, LANE), wall_mask[1, z, x])
                 eq_z = equilibrium[z * rows : (z + 1) * rows]
                 ghost_low = jnp.where(mask_low == 1, mirrored[low : low + 1], eq_z[0:1])
                 ghost_high = jnp.where(
                     mask_high == 1, mirrored[high : high + 1], eq_z[rows - 1 : rows]
                 )
-                below = pltpu.roll(values[z], 1, axis=0)
-                above = pltpu.roll(values[z], rows - 1, axis=0)
-                below = jnp.where(row_index == 0, ghost_low, below)
-                above = jnp.where(row_index == rows - 1, ghost_high, above)
-                side = jnp.where(pos2, below, above)
-                before, after = values[(z - 1) % planes], values[(z + 1) % planes]
-                if (z - 1) % planes == (z + 1) % planes:
-                    plane = before
-                else:
-                    plane = jnp.where(pos3, before, after)
-                parts.append(coef_f * values[z] + coef_y * side + coef_z * plane)
-            b_list.append((jnp.concatenate(parts, axis=0) + source) * inverse)
+                flux = sb_ref[j, x, z * rows : (z + 1) * rows, :]
+                parts += [
+                    flux[:8] + jnp.where(group_index == 0, coef_low * ghost_low, 0.0),
+                    flux[8 : rows - 8],
+                    flux[rows - 8 :] + jnp.where(group_index == 7, coef_high * ghost_high, 0.0),
+                ]
+            b_list.append((jnp.concatenate(parts, axis=0) + rates * equilibrium) * inverse)
             a_list.append(sigma * inverse)
             if x in (0, depth - 1):
                 eq_list.append(equilibrium)
@@ -416,12 +436,7 @@
         face_copy(c).start()
         return carry
 
-    def own_block(c, carry):
-        local_block(own0 + c)
-        return carry
-
     lax.fori_loop(0, half_blocks, far_block, 0)
-    lax.fori_loop(0, half_blocks, own_block, 0)
 
     rate_copy().wait()
     prate_ref[...] = jnp.broadcast_to(rate_recv[0:1, :], (LANE, cells)).T
@@ -431,8 +446,9 @@
         sign = jnp.where(x1 > 0, 1.0, -1.0)
         return sign * jnp.where(q == 0, 1.0, -1.0) > 0
 
-    def pair_block(c, carry):
+    def pair_block(c):
         j = own0 + c
+        local_block(j)
         x1, _, _ = block_tables(j)
         sigma = stream_x * jnp.abs(x1)
         opening = 1.0 + sigma
@@ -448,9 +464,6 @@
         pair_a[c, 0] = other
         pair_a[c, 1] = a_own * other
         pair_b[c] = jnp.where(first, other * b_own + b_other, a_own * b_other + b_own)
-        return carry
-
-    lax.fori_loop(0, half_blocks, pair_block, 0)
 
     def down_copy(c):
         return pltpu.make_async_remote_copy(
@@ -497,6 +510,10 @@
         c_dn = t - p
         c_up = t - back
         c_end = t - latest
+
+        @pl.when(t < half_blocks)
+        def _():
+            pair_block(t)
 
         @pl.when((c_dn >= 0) & (c_dn < half_blocks))
         def _():
@@ -650,9 +667,9 @@
         ]
         + [pltpu.SemaphoreType.DMA((half,))] * 8,
         compiler_params=pltpu.CompilerParams(
-            collective_id=0, has_side_effects=True, vmem_limit_bytes=40 * 1024 * 1024
+            collective_id=0, has_side_effects=True, vmem_limit_bytes=62 * 1024 * 1024
         ),
-    )(wall_mask, grid_point.reshape(blocks, LANE), mirror_slot.reshape(blocks, LANE), flat)
+    )(wall_mask.transpose(1, 2, 0), grid_point.reshape(blocks, LANE), mirror_slot.reshape(blocks, LANE), flat)
     return (
         out.reshape(depth, rows, blocks, planes, LANE)
         .transpose(0, 1, 3, 2, 4)

time: 38.5 us -> 38.1 us (0.990)
  local copies, waits for them, and re-layouts: 2.98 us -> 2.29 us
    unnamed x10 -> x1, local copies, waits for them, and re-layouts: 2.98 us -> 2.29 us
where the time goes in v3:
time: 38.1 us; the launch traced here: 37.9 us
  Pallas kernels  35.6 us (93%)
  local copies, waits for them, and re-layouts  2.29 us (6%)
    pallas_call x1, Pallas kernels, shards(): pl.pallas_call(functools.partial(kernel, dims), out_shape=jax.ShapeDtypeS...  35.6 us
    unnamed x1, local copies, waits for them, and re-layouts  2.29 us

profile of v3, /device:TPU:0, one launch (start us, length us, event | category | flops | bytes accessed | tf_op | source)
XLA Modules:
  0.0 37.9 jit_solution(15513377274592954847)
XLA Ops:
  0.0 35.6 %shard_map.46 = f32[2048,128]{1,0:T(8,128)} custom-call(s32[2,2,4]{2,1,0:T(2,128)} %bitcast.17, s32[8,128]{1,0:T(8,128)} %bitcast.15, s32[8,128]{1,0:T(8,128)} %bitcast.16, f32[2048,128]{1,0:T(8,128)} %bitcast.14), custom_call_target="tpu_custom_call" | custom-call | tf_op jit(solution)/shard_map/pallas_call | solution.py:620
  35.6 2.3 %copy.8 = f32[4,32,2,1024]{3,2,1,0:T(2,128)} copy(f32[4,32,2,1024]{3,2,1,0:T(2,128)} %bitcast.13) | data formatting | bytes 2097152

commit v4 on v3

--- a/solution.py
+++ b/solution.py
@@ -52,9 +52,8 @@
     wall_mask,
     grid_ref,
     mirror_ref,
-    f_hbm,
+    f_ref,
     out_ref,
-    f_ref,
     wall_ref,
     wsplit_ref,
     pick_ref,
@@ -84,7 +83,6 @@
     enter_own,
     enter_send,
     enter_recv,
-    f_sem,
     wall_ssem,
     wall_rsem,
     mom_ssem,
@@ -118,9 +116,6 @@
 
     def frow(x, y, j, z):
         return (x * rows + y) * stride + j * planes + z
-
-    load = pltpu.make_async_copy(f_hbm, f_ref, f_sem)
-    load.start()
 
     barrier = pltpu.get_barrier_semaphore()
     for d in range(1, nvel):
@@ -166,8 +161,6 @@
         index = lax.broadcasted_iota(jnp.int32, (2 * LANE, LANE), 0) & (LANE - 1)
         pick_ref[j] = jnp.where(index == (slot & (LANE - 1)), 1.0, 0.0).astype(BF16)
 
-    load.wait()
-
     for x in range(depth):
         for w in range(2):
             for z in range(planes):
@@ -176,52 +169,6 @@
                 wall_ref[v, pl.ds(r, blocks, stride=walls), :] = f_ref[
                     pl.ds(frow(x, y, 0, z), blocks, stride=planes), :
                 ]
-
-    greetings = nvel + (p > 0).astype(jnp.int32) + (p < pairs - 1).astype(jnp.int32)
-    pl.semaphore_wait(barrier, greetings)
-
-    sibling = v + 1 - 2 * lax.rem(v, 2)
-    twins = nvel // 2
-
-    def far(base, m):
-        return lax.rem(base + 2 * m + nvel, nvel)
-
-    def wall_copy(k, origin, target):
-        return pltpu.make_async_remote_copy(
-            src_ref=wall_ref.at[origin],
-            dst_ref=wall_ref.at[origin],
-            send_sem=wall_ssem.at[k],
-            recv_sem=wall_rsem.at[k],
-            device_id=(s, target),
-            device_id_type=MESH,
-        )
-
-    def wall_far(m):
-        return wall_copy(m, v, far(v, m))
-
-    def wall_far_arrival(m):
-        return wall_copy(m, far(v, -m), far(v, m))
-
-    def wall_forward(m):
-        return wall_copy(twins - 1 + m, far(v, -m), sibling)
-
-    def wall_forward_arrival(m):
-        return wall_copy(twins - 1 + m, far(sibling, -m), sibling)
-
-    def mom_copy(k):
-        target = far(v if k % 2 == 0 else sibling, k // 2)
-        return pltpu.make_async_remote_copy(
-            src_ref=mom_ref.at[0],
-            dst_ref=mom_ref.at[k],
-            send_sem=mom_ssem.at[k - 1],
-            recv_sem=mom_rsem.at[k - 1],
-            device_id=(s, target),
-            device_id_type=MESH,
-        )
-
-    for m in range(1, twins):
-        wall_far(m).start()
-    wall_copy(0, v, sibling).start()
 
     for x in range(depth):
         for z in range(planes):
@@ -233,6 +180,53 @@
                 cell_ref[j, x, z * rows : (z + 1) * rows, :] = part
                 fhi_ref[base : base + rows, j * LANE : (j + 1) * LANE] = hi
                 flo_ref[base : base + rows, j * LANE : (j + 1) * LANE] = lo
+
+    greetings = nvel + (p > 0).astype(jnp.int32) + (p < pairs - 1).astype(jnp.int32)
+    pl.semaphore_wait(barrier, greetings)
+
+    sibling = v + 1 - 2 * lax.rem(v, 2)
+    twins = nvel // 2
+
+    def far(base, m):
+        return lax.rem(base + 2 * m + nvel, nvel)
+
+    def wall_copy(k, origin, target):
+        return pltpu.make_async_remote_copy(
+            src_ref=wall_ref.at[origin],
+            dst_ref=wall_ref.at[origin],
+            send_sem=wall_ssem.at[k],
+            recv_sem=wall_rsem.at[k],
+            device_id=(s, target),
+            device_id_type=MESH,
+        )
+
+    def wall_far(m):
+        return wall_copy(m, v, far(v, m))
+
+    def wall_far_arrival(m):
+        return wall_copy(m, far(v, -m), far(v, m))
+
+    def wall_forward(m):
+        return wall_copy(twins - 1 + m, far(v, -m), sibling)
+
+    def wall_forward_arrival(m):
+        return wall_copy(twins - 1 + m, far(sibling, -m), sibling)
+
+    def mom_copy(k):
+        target = far(v if k % 2 == 0 else sibling, k // 2)
+        return pltpu.make_async_remote_copy(
+            src_ref=mom_ref.at[0],
+            dst_ref=mom_ref.at[k],
+            send_sem=mom_ssem.at[k - 1],
+            recv_sem=mom_rsem.at[k - 1],
+            device_id=(s, target),
+            device_id_type=MESH,
+        )
+
+    for m in range(1, twins):
+        wall_far(m).start()
+    wall_copy(0, v, sibling).start()
+
     contract = (((1,), (1,)), ((), ()))
     sums = lax.dot_general(
         fhi_ref[...], tmom_ref[...], contract, preferred_element_type=F32
@@ -421,19 +415,23 @@
             sa_ref[j, k] = a_run
             sb_ref[j, k] = b_run
 
-    def face_copy(c):
+    def band(z):
+        return pl.ds(z * rows, rows)
+
+    def face_copy(c, z):
         return pltpu.make_async_remote_copy(
-            src_ref=sb_ref.at[far0 + c, depth - 1],
-            dst_ref=pb_ref.at[c],
-            send_sem=face_ssem.at[c],
-            recv_sem=face_rsem.at[c],
+            src_ref=sb_ref.at[far0 + c, depth - 1, band(z)],
+            dst_ref=pb_ref.at[c, band(z)],
+            send_sem=face_ssem.at[c, z],
+            recv_sem=face_rsem.at[c, z],
             device_id=(partner, v),
             device_id_type=MESH,
         )
 
     def far_block(c, carry):
         local_block(far0 + c)
-        face_copy(c).start()
+        for z in range(planes):
+            face_copy(c, z).start()
         return carry
 
     lax.fori_loop(0, half_blocks, far_block, 0)
@@ -456,7 +454,8 @@
         for x in range(depth):
             a = sigma / (opening + prate_ref[x * cells_x : (x + 1) * cells_x, :])
             other = a if other is None else other * a
-        face_copy(c).wait_recv()
+        for z in range(planes):
+            face_copy(c, z).wait_recv()
         a_own = sa_ref[j, depth - 1]
         b_own = sb_ref[j, depth - 1]
         b_other = pb_ref[c]
@@ -465,32 +464,32 @@
         pair_a[c, 1] = a_own * other
         pair_b[c] = jnp.where(first, other * b_own + b_other, a_own * b_other + b_own)
 
-    def down_copy(c):
+    def down_copy(c, z):
         return pltpu.make_async_remote_copy(
-            src_ref=od_ref.at[c],
-            dst_ref=ed_ref.at[c],
-            send_sem=dn_ssem.at[c],
-            recv_sem=dn_rsem.at[c],
+            src_ref=od_ref.at[c, band(z)],
+            dst_ref=ed_ref.at[c, band(z)],
+            send_sem=dn_ssem.at[c, z],
+            recv_sem=dn_rsem.at[c, z],
             device_id=(s + 2, v),
             device_id_type=MESH,
         )
 
-    def up_copy(c):
+    def up_copy(c, z):
         return pltpu.make_async_remote_copy(
-            src_ref=ou_ref.at[c],
-            dst_ref=eu_ref.at[c],
-            send_sem=up_ssem.at[c],
-            recv_sem=up_rsem.at[c],
+            src_ref=ou_ref.at[c, band(z)],
+            dst_ref=eu_ref.at[c, band(z)],
+            send_sem=up_ssem.at[c, z],
+            recv_sem=up_rsem.at[c, z],
             device_id=(s - 2, v),
             device_id_type=MESH,
         )
 
-    def return_copy(c):
+    def return_copy(c, z):
         return pltpu.make_async_remote_copy(
-            src_ref=enter_send.at[c],
-            dst_ref=enter_recv.at[c],
-            send_sem=ret_ssem.at[c],
-            recv_sem=ret_rsem.at[c],
+            src_ref=enter_send.at[c, band(z)],
+            dst_ref=enter_recv.at[c, band(z)],
+            send_sem=ret_ssem.at[c, z],
+            recv_sem=ret_rsem.at[c, z],
             device_id=(partner, v),
             device_id_type=MESH,
         )
@@ -517,37 +516,46 @@
 
         @pl.when((c_dn >= 0) & (c_dn < half_blocks))
         def _():
-            @pl.when(p > 0)
-            def _():
-                down_copy(c_dn).wait_recv()
-
-            @pl.when(p < pairs - 1)
-            def _():
-                od_ref[c_dn] = pair_a[c_dn, 1] * ed_ref[c_dn] + pair_b[c_dn]
-                down_copy(c_dn).start()
+            for z in range(planes):
+                at = (c_dn, band(z))
+
+                @pl.when(p > 0)
+                def _():
+                    down_copy(c_dn, z).wait_recv()
+
+                @pl.when(p < pairs - 1)
+                def _():
+                    od_ref[at] = pair_a[c_dn, 1, band(z)] * ed_ref[at] + pair_b[at]
+                    down_copy(c_dn, z).start()
 
         @pl.when((c_up >= 0) & (c_up < half_blocks))
         def _():
-            @pl.when(p < pairs - 1)
-            def _():
-                up_copy(c_up).wait_recv()
-
-            @pl.when(p > 0)
-            def _():
-                ou_ref[c_up] = pair_a[c_up, 1] * eu_ref[c_up] + pair_b[c_up]
-                up_copy(c_up).start()
+            for z in range(planes):
+                at = (c_up, band(z))
+
+                @pl.when(p < pairs - 1)
+                def _():
+                    up_copy(c_up, z).wait_recv()
+
+                @pl.when(p > 0)
+                def _():
+                    ou_ref[at] = pair_a[c_up, 1, band(z)] * eu_ref[at] + pair_b[at]
+                    up_copy(c_up, z).start()
 
         @pl.when((c_end >= 0) & (c_end < half_blocks))
         def _():
             j = own0 + c_end
             x1, _, _ = block_tables(j)
-            enter = jnp.where(x1 > 0, ed_ref[c_end], eu_ref[c_end])
             first = first_weight(x1)
-            after_own = sa_ref[j, depth - 1] * enter + sb_ref[j, depth - 1]
-            after_other = pair_a[c_end, 0] * enter + pb_ref[c_end]
-            enter_send[c_end] = jnp.where(first, after_own, enter)
-            return_copy(c_end).start()
-            enter_own[c_end] = jnp.where(first, enter, after_other)
+            for z in range(planes):
+                at = (c_end, band(z))
+                enter = jnp.where(x1 > 0, ed_ref[at], eu_ref[at])
+                last = (j, depth - 1, band(z))
+                after_own = sa_ref[last] * enter + sb_ref[last]
+                after_other = pair_a[c_end, 0, band(z)] * enter + pb_ref[at]
+                enter_send[at] = jnp.where(first, after_own, enter)
+                return_copy(c_end, z).start()
+                enter_own[at] = jnp.where(first, enter, after_other)
 
         return carry
 
@@ -569,7 +577,8 @@
         return carry
 
     def finish_far(c, carry):
-        return_copy(c).wait_recv()
+        for z in range(planes):
+            return_copy(c, z).wait_recv()
         finish(far0 + c, enter_recv[c])
         return carry
 
@@ -584,16 +593,17 @@
         mom_copy(d).wait_send()
 
     def drain(c, carry):
-        face_copy(c).wait_send()
-        return_copy(c).wait_send()
-
-        @pl.when(p < pairs - 1)
-        def _():
-            down_copy(c).wait_send()
-
-        @pl.when(p > 0)
-        def _():
-            up_copy(c).wait_send()
+        for z in range(planes):
+            face_copy(c, z).wait_send()
+            return_copy(c, z).wait_send()
+
+            @pl.when(p < pairs - 1)
+            def _():
+                down_copy(c, z).wait_send()
+
+            @pl.when(p > 0)
+            def _():
+                up_copy(c, z).wait_send()
 
         return carry
 
@@ -624,11 +634,10 @@
             pl.BlockSpec(memory_space=pltpu.SMEM),
             vmem,
             vmem,
-            pl.BlockSpec(memory_space=pl.ANY),
+            vmem,
         ],
         out_specs=vmem,
         scratch_shapes=[
-            pltpu.VMEM((count, LANE), F32),
             pltpu.VMEM((nvel, blocks * walls, LANE), F32),
             pltpu.VMEM((nvel * blocks * walls, 2 * LANE), BF16),
             pltpu.VMEM((blocks, 2 * LANE, LANE), BF16),
@@ -658,16 +667,15 @@
             pltpu.VMEM(face, F32),
             pltpu.VMEM(face, F32),
             pltpu.VMEM(face, F32),
-            pltpu.SemaphoreType.DMA,
             pltpu.SemaphoreType.DMA((nvel - 1,)),
             pltpu.SemaphoreType.DMA((nvel - 1,)),
             pltpu.SemaphoreType.DMA((nvel - 1,)),
             pltpu.SemaphoreType.DMA((nvel - 1,)),
             pltpu.SemaphoreType.DMA((2,)),
         ]
-        + [pltpu.SemaphoreType.DMA((half,))] * 8,
+        + [pltpu.SemaphoreType.DMA((half, planes))] * 8,
         compiler_params=pltpu.CompilerParams(
-            collective_id=0, has_side_effects=True, vmem_limit_bytes=62 * 1024 * 1024
+            collective_id=0, has_side_effects=True, vmem_limit_bytes=40 * 1024 * 1024
         ),
     )(wall_mask.transpose(1, 2, 0), grid_point.reshape(blocks, LANE), mirror_slot.reshape(blocks, LANE), flat)
     return (

time: 38.1 us -> 37.6 us (0.987)
  Pallas kernels: 35.6 us -> 33.8 us
  local copies, waits for them, and re-layouts: 2.29 us -> 3.58 us
    pallas_call x1, Pallas kernels: 35.6 us -> 33.8 us  [shards(): pl.pallas_call(functools.partial(kernel, dims), out_shape=jax.ShapeDtypeS...]
    unnamed x1 -> x9, local copies, waits for them, and re-layouts: 2.29 us -> 3.58 us
where the time goes in v4:
time: 37.6 us; the launch traced here: 37.4 us
  Pallas kernels  33.8 us (90%)
  local copies, waits for them, and re-layouts  3.58 us (10%)
    pallas_call x1, Pallas kernels, shards(): pl.pallas_call(functools.partial(kernel, dims), out_shape=jax.ShapeDtypeS...  33.8 us
    unnamed x9, local copies, waits for them, and re-layouts  3.58 us

profile of v4, /device:TPU:0, one launch (start us, length us, event | category | flops | bytes accessed | tf_op | source)
XLA Modules:
  0.0 37.4 jit_solution(18243558499294480938)
XLA Ops:
  0.0 0.0 copy-start.1
  0.0 0.0 copy-start.3
  0.0 0.7 %copy-done.1 = s32[1024]{0:T(1024)S(1)} copy-done((s32[1024]{0:T(1024)S(1)}, s32[1024]{0:T(1024)}, u32[]{:S(2)}) %copy-start.1) | copy-done | bytes 4120
  0.7 0.0 copy-done.3
  0.7 0.0 copy-start
  0.7 1.2 %copy-done = f32[4,32,2,1024]{3,2,1,0:T(2,128)S(1)} copy-done((f32[4,32,2,1024]{3,2,1,0:T(2,128)S(1)}, f32[4,32,2,1024]{3,2,1,0:T(2,128)}, u32[]{:S(2)}) %copy-start) | copy-done | bytes 1048600
  1.9 0.0 copy-start.2
  1.9 0.7 %copy-done.2 = s32[1024]{0:T(1024)S(1)} copy-done((s32[1024]{0:T(1024)S(1)}, s32[1024]{0:T(1024)}, u32[]{:S(2)}) %copy-start.2) | copy-done | bytes 4120
  2.6 33.8 %shard_map.46 = f32[2048,128]{1,0:T(8,128)S(1)} custom-call(s32[2,2,4]{2,1,0:T(2,128)S(1)} %bitcast.17, s32[8,128]{1,0:T(8,128)S(1)} %bitcast.15, s32[8,128]{1,0:T(8,128)S(1)} %bitcast.16, f32[2048,128]{1,0:T(8,128)S(1)} %bitcast.14), custom_call_target="tpu_custom_call" | custom-call | tf_op jit(solution)/shard_map/pallas_call | solution.py:630
  36.4 1.0 %copy.8 = f32[4,32,2,1024]{3,2,1,0:T(2,128)} copy(f32[4,32,2,1024]{3,2,1,0:T(2,128)S(1)} %bitcast.13) | data formatting | bytes 2097152
Async XLA Ops:
  0.0 0.7 %copy-start.1 = (s32[1024]{0:T(1024)S(1)}, s32[1024]{0:T(1024)}, u32[]{:S(2)}) copy-start(s32[1024]{0:T(1024)} %param.6) | copy-start | bytes 12292
  0.0 0.7 %copy-start.3 = (s32[4,2,2]{0,2,1:T(2,128)S(1)}, s32[4,2,2]{0,2,1:T(2,128)}, u32[]{:S(2)}) copy-start(s32[4,2,2]{0,2,1:T(2,128)} %param.5) | copy-start | bytes 196
  0.7 1.2 %copy-start = (f32[4,32,2,1024]{3,2,1,0:T(2,128)S(1)}, f32[4,32,2,1024]{3,2,1,0:T(2,128)}, u32[]{:S(2)}) copy-start(f32[4,32,2,1024]{3,2,1,0:T(2,128)} %param.4) | copy-start | bytes 3145732
  1.9 0.7 %copy-start.2 = (s32[1024]{0:T(1024)S(1)}, s32[1024]{0:T(1024)}, u32[]{:S(2)}) copy-start(s32[1024]{0:T(1024)} %param.7) | copy-start | bytes 12292

commit v5 on v4

--- a/solution.py
+++ b/solution.py
@@ -52,8 +52,9 @@
     wall_mask,
     grid_ref,
     mirror_ref,
+    f_hbm,
+    out_ref,
     f_ref,
-    out_ref,
     wall_ref,
     wsplit_ref,
     pick_ref,
@@ -83,6 +84,7 @@
     enter_own,
     enter_send,
     enter_recv,
+    f_sem,
     wall_ssem,
     wall_rsem,
     mom_ssem,
@@ -116,6 +118,9 @@
 
     def frow(x, y, j, z):
         return (x * rows + y) * stride + j * planes + z
+
+    load = pltpu.make_async_copy(f_hbm, f_ref, f_sem)
+    load.start()
 
     barrier = pltpu.get_barrier_semaphore()
     for d in range(1, nvel):
@@ -160,6 +165,8 @@
         slot = mirror_ref[j : j + 1, :]
         index = lax.broadcasted_iota(jnp.int32, (2 * LANE, LANE), 0) & (LANE - 1)
         pick_ref[j] = jnp.where(index == (slot & (LANE - 1)), 1.0, 0.0).astype(BF16)
+
+    load.wait()
 
     for x in range(depth):
         for w in range(2):
@@ -432,9 +439,15 @@
         local_block(far0 + c)
         for z in range(planes):
             face_copy(c, z).start()
+
+        @pl.when(c > 0)
+        def _():
+            local_block(own0 + c - 1)
+
         return carry
 
     lax.fori_loop(0, half_blocks, far_block, 0)
+    local_block(own0 + half_blocks - 1)
 
     rate_copy().wait()
     prate_ref[...] = jnp.broadcast_to(rate_recv[0:1, :], (LANE, cells)).T
@@ -446,7 +459,6 @@
 
     def pair_block(c):
         j = own0 + c
-        local_block(j)
         x1, _, _ = block_tables(j)
         sigma = stream_x * jnp.abs(x1)
         opening = 1.0 + sigma
@@ -634,10 +646,11 @@
             pl.BlockSpec(memory_space=pltpu.SMEM),
             vmem,
             vmem,
-            vmem,
+            pl.BlockSpec(memory_space=pl.ANY),
         ],
         out_specs=vmem,
         scratch_shapes=[
+            pltpu.VMEM((count, LANE), F32),
             pltpu.VMEM((nvel, blocks * walls, LANE), F32),
             pltpu.VMEM((nvel * blocks * walls, 2 * LANE), BF16),
             pltpu.VMEM((blocks, 2 * LANE, LANE), BF16),
@@ -667,6 +680,7 @@
             pltpu.VMEM(face, F32),
             pltpu.VMEM(face, F32),
             pltpu.VMEM(face, F32),
+            pltpu.SemaphoreType.DMA,
             pltpu.SemaphoreType.DMA((nvel - 1,)),
             pltpu.SemaphoreType.DMA((nvel - 1,)),
             pltpu.SemaphoreType.DMA((nvel - 1,)),
@@ -675,7 +689,7 @@
         ]
         + [pltpu.SemaphoreType.DMA((half, planes))] * 8,
         compiler_params=pltpu.CompilerParams(
-            collective_id=0, has_side_effects=True, vmem_limit_bytes=40 * 1024 * 1024
+            collective_id=0, has_side_effects=True, vmem_limit_bytes=62 * 1024 * 1024
         ),
     )(wall_mask.transpose(1, 2, 0), grid_point.reshape(blocks, LANE), mirror_slot.reshape(blocks, LANE), flat)
     return (

time: 37.6 us -> 37.7 us (level)
  Pallas kernels: 33.8 us -> 35.2 us
  local copies, waits for them, and re-layouts: 3.58 us -> 2.29 us
    pallas_call x1, Pallas kernels: 33.8 us -> 35.2 us  [shards(): pl.pallas_call(functools.partial(kernel, dims), out_shape=jax.ShapeDtypeS...]
    unnamed x9 -> x1, local copies, waits for them, and re-layouts: 3.58 us -> 2.29 us
where the time goes in v5:
time: 37.7 us; the launch traced here: 37.5 us
  Pallas kernels  35.2 us (93%)
  local copies, waits for them, and re-layouts  2.29 us (6%)
    pallas_call x1, Pallas kernels, shards(): pl.pallas_call(functools.partial(kernel, dims), out_shape=jax.ShapeDtypeS...  35.2 us
    unnamed x1, local copies, waits for them, and re-layouts  2.29 us

profile of v5, /device:TPU:0, one launch (start us, length us, event | category | flops | bytes accessed | tf_op | source)
XLA Modules:
  0.0 37.5 jit_solution(4385778671581027926)
XLA Ops:
  0.0 35.2 %shard_map.46 = f32[2048,128]{1,0:T(8,128)} custom-call(s32[2,2,4]{2,1,0:T(2,128)} %bitcast.17, s32[8,128]{1,0:T(8,128)} %bitcast.15, s32[8,128]{1,0:T(8,128)} %bitcast.16, f32[2048,128]{1,0:T(8,128)} %bitcast.14), custom_call_target="tpu_custom_call" | custom-call | tf_op jit(solution)/shard_map/pallas_call | solution.py:642
  35.2 2.3 %copy.8 = f32[4,32,2,1024]{3,2,1,0:T(2,128)} copy(f32[4,32,2,1024]{3,2,1,0:T(2,128)} %bitcast.13) | data formatting | bytes 2097152

commit v6 on v5

--- a/solution.py
+++ b/solution.py
@@ -514,6 +514,17 @@
     def _():
         eu_ref[...] = jnp.zeros_like(eu_ref)
 
+    def finish(j, enter):
+        x1, _, _ = block_tables(j)
+        pos1 = x1 > 0
+        done = [sa_ref[j, k] * enter + sb_ref[j, k] for k in range(depth)]
+        for x in range(depth):
+            value = jnp.where(pos1, done[x], done[depth - 1 - x])
+            for z in range(planes):
+                out_ref[pl.ds(frow(x, 0, j, z), rows, stride=stride), :] = value[
+                    z * rows : (z + 1) * rows
+                ]
+
     back = pairs - 1 - p
     latest = jnp.maximum(p, back)
 
@@ -568,25 +579,11 @@
                 enter_send[at] = jnp.where(first, after_own, enter)
                 return_copy(c_end, z).start()
                 enter_own[at] = jnp.where(first, enter, after_other)
+            finish(j, enter_own[c_end])
 
         return carry
 
     lax.fori_loop(0, half_blocks + pairs - 1, chain_step, 0)
-
-    def finish(j, enter):
-        x1, _, _ = block_tables(j)
-        pos1 = x1 > 0
-        done = [sa_ref[j, k] * enter + sb_ref[j, k] for k in range(depth)]
-        for x in range(depth):
-            value = jnp.where(pos1, done[x], done[depth - 1 - x])
-            for z in range(planes):
-                out_ref[pl.ds(frow(x, 0, j, z), rows, stride=stride), :] = value[
-                    z * rows : (z + 1) * rows
-                ]
-
-    def finish_own(c, carry):
-        finish(own0 + c, enter_own[c])
-        return carry
 
     def finish_far(c, carry):
         for z in range(planes):
@@ -594,7 +591,6 @@
         finish(far0 + c, enter_recv[c])
         return carry
 
-    lax.fori_loop(0, half_blocks, finish_own, 0)
     lax.fori_loop(0, half_blocks, finish_far, 0)
 
     wall_copy(0, v, sibling).wait_send()

time: 37.7 us -> 37.7 us (level)
  no operation moved by 1% of the time
where the time goes in v6:
time: 37.7 us; the launch traced here: 37.5 us
  Pallas kernels  35.2 us (93%)
  local copies, waits for them, and re-layouts  2.29 us (6%)
    pallas_call x1, Pallas kernels, shards(): pl.pallas_call(functools.partial(kernel, dims), out_shape=jax.ShapeDtypeS...  35.2 us
    unnamed x1, local copies, waits for them, and re-layouts  2.29 us

profile of v6, /device:TPU:0, one launch (start us, length us, event | category | flops | bytes accessed | tf_op | source)
XLA Modules:
  0.0 37.5 jit_solution(6382474195251696675)
XLA Ops:
  0.0 35.2 %shard_map.46 = f32[2048,128]{1,0:T(8,128)} custom-call(s32[2,2,4]{2,1,0:T(2,128)} %bitcast.17, s32[8,128]{1,0:T(8,128)} %bitcast.15, s32[8,128]{1,0:T(8,128)} %bitcast.16, f32[2048,128]{1,0:T(8,128)} %bitcast.14), custom_call_target="tpu_custom_call" | custom-call | tf_op jit(solution)/shard_map/pallas_call | solution.py:638
  35.2 2.3 %copy.8 = f32[4,32,2,1024]{3,2,1,0:T(2,128)} copy(f32[4,32,2,1024]{3,2,1,0:T(2,128)} %bitcast.13) | data formatting | bytes 2097152

commit v7 on v6

--- a/solution.py
+++ b/solution.py
@@ -52,9 +52,8 @@
     wall_mask,
     grid_ref,
     mirror_ref,
-    f_hbm,
+    f_ref,
     out_ref,
-    f_ref,
     wall_ref,
     wsplit_ref,
     pick_ref,
@@ -84,7 +83,6 @@
     enter_own,
     enter_send,
     enter_recv,
-    f_sem,
     wall_ssem,
     wall_rsem,
     mom_ssem,
@@ -118,9 +116,6 @@
 
     def frow(x, y, j, z):
         return (x * rows + y) * stride + j * planes + z
-
-    load = pltpu.make_async_copy(f_hbm, f_ref, f_sem)
-    load.start()
 
     barrier = pltpu.get_barrier_semaphore()
     for d in range(1, nvel):
@@ -165,8 +160,6 @@
         slot = mirror_ref[j : j + 1, :]
         index = lax.broadcasted_iota(jnp.int32, (2 * LANE, LANE), 0) & (LANE - 1)
         pick_ref[j] = jnp.where(index == (slot & (LANE - 1)), 1.0, 0.0).astype(BF16)
-
-    load.wait()
 
     for x in range(depth):
         for w in range(2):
@@ -391,8 +384,8 @@
             for z in range(planes):
                 low = (x * 2) * planes + z
                 high = (x * 2 + 1) * planes + z
-                mask_low = jnp.full((1, LANE), wall_mask[0, z, x])
-                mask_high = jnp.full((1, LANE), wall_mask[1, z, x])
+                mask_low = jnp.full((1, LANE), wall_mask[x, 0, z])
+                mask_high = jnp.full((1, LANE), wall_mask[x, 1, z])
                 eq_z = equilibrium[z * rows : (z + 1) * rows]
                 ghost_low = jnp.where(mask_low == 1, mirrored[low : low + 1], eq_z[0:1])
                 ghost_high = jnp.where(
@@ -439,15 +432,9 @@
         local_block(far0 + c)
         for z in range(planes):
             face_copy(c, z).start()
-
-        @pl.when(c > 0)
-        def _():
-            local_block(own0 + c - 1)
-
         return carry
 
     lax.fori_loop(0, half_blocks, far_block, 0)
-    local_block(own0 + half_blocks - 1)
 
     rate_copy().wait()
     prate_ref[...] = jnp.broadcast_to(rate_recv[0:1, :], (LANE, cells)).T
@@ -459,6 +446,7 @@
 
     def pair_block(c):
         j = own0 + c
+        local_block(j)
         x1, _, _ = block_tables(j)
         sigma = stream_x * jnp.abs(x1)
         opening = 1.0 + sigma
@@ -642,11 +630,10 @@
             pl.BlockSpec(memory_space=pltpu.SMEM),
             vmem,
             vmem,
-            pl.BlockSpec(memory_space=pl.ANY),
+            vmem,
         ],
         out_specs=vmem,
         scratch_shapes=[
-            pltpu.VMEM((count, LANE), F32),
             pltpu.VMEM((nvel, blocks * walls, LANE), F32),
             pltpu.VMEM((nvel * blocks * walls, 2 * LANE), BF16),
             pltpu.VMEM((blocks, 2 * LANE, LANE), BF16),
@@ -676,7 +663,6 @@
             pltpu.VMEM(face, F32),
             pltpu.VMEM(face, F32),
             pltpu.VMEM(face, F32),
-            pltpu.SemaphoreType.DMA,
             pltpu.SemaphoreType.DMA((nvel - 1,)),
             pltpu.SemaphoreType.DMA((nvel - 1,)),
             pltpu.SemaphoreType.DMA((nvel - 1,)),
@@ -685,9 +671,9 @@
         ]
         + [pltpu.SemaphoreType.DMA((half, planes))] * 8,
         compiler_params=pltpu.CompilerParams(
-            collective_id=0, has_side_effects=True, vmem_limit_bytes=62 * 1024 * 1024
+            collective_id=0, has_side_effects=True, vmem_limit_bytes=40 * 1024 * 1024
         ),
-    )(wall_mask.transpose(1, 2, 0), grid_point.reshape(blocks, LANE), mirror_slot.reshape(blocks, LANE), flat)
+    )(wall_mask, grid_point.reshape(blocks, LANE), mirror_slot.reshape(blocks, LANE), flat)
     return (
         out.reshape(depth, rows, blocks, planes, LANE)
         .transpose(0, 1, 3, 2, 4)

time: 37.7 us -> 37 us (0.981)
  Pallas kernels: 35.2 us -> 33.8 us
  local copies, waits for them, and re-layouts: 2.29 us -> 2.98 us
    pallas_call x1, Pallas kernels: 35.2 us -> 33.8 us  [shards(): pl.pallas_call(functools.partial(kernel, dims), out_shape=jax.ShapeDtypeS...]
    unnamed x1 -> x10, local copies, waits for them, and re-layouts: 2.29 us -> 2.98 us
where the time goes in v7:
time: 37 us; the launch traced here: 36.8 us
  Pallas kernels  33.8 us (91%)
  local copies, waits for them, and re-layouts  2.98 us (8%)
    pallas_call x1, Pallas kernels, shards(): pl.pallas_call(functools.partial(kernel, dims), out_shape=jax.ShapeDtypeS...  33.8 us
    unnamed x10, local copies, waits for them, and re-layouts  2.98 us

profile of v7, /device:TPU:0, one launch (start us, length us, event | category | flops | bytes accessed | tf_op | source)
XLA Modules:
  0.0 36.8 jit_solution(4174196308871171011)
XLA Ops:
  0.0 0.0 copy-start.3
  0.0 0.0 copy-start.2
  0.0 0.0 copy-start.1
  0.0 0.7 %copy-done.3 = s32[4,2,2]{0,2,1:T(2,128)S(1)} copy-done((s32[4,2,2]{0,2,1:T(2,128)S(1)}, s32[4,2,2]{0,2,1:T(2,128)}, u32[]{:S(2)}) %copy-start.3) | copy-done | bytes 88
  0.7 0.1 copy.6.wall_mask
  0.8 0.0 copy-done.2
  0.8 0.0 copy-done.1
  0.8 0.0 copy-start
  0.8 1.2 %copy-done = f32[4,32,2,1024]{3,2,1,0:T(2,128)S(1)} copy-done((f32[4,32,2,1024]{3,2,1,0:T(2,128)S(1)}, f32[4,32,2,1024]{3,2,1,0:T(2,128)}, u32[]{:S(2)}) %copy-start) | copy-done | bytes 1048600
  2.0 33.8 %shard_map.46 = f32[2048,128]{1,0:T(8,128)S(1)} custom-call(s32[4,2,2]{2,1,0:T(2,128)S(1)} %copy.6.wall_mask, s32[8,128]{1,0:T(8,128)S(1)} %bitcast.14, s32[8,128]{1,0:T(8,128)S(1)} %bitcast.15, f32[2048,128]{1,0:T(8,128)S(1)} %bitcast.13), custom_call_target="tpu_custom_call" | custom-call | tf_op jit(solution)/shard_map/pallas_call | solution.py:626
  35.8 1.0 %copy.9 = f32[4,32,2,1024]{3,2,1,0:T(2,128)} copy(f32[4,32,2,1024]{3,2,1,0:T(2,128)S(1)} %bitcast.12) | data formatting | bytes 2097152
Async XLA Ops:
  0.0 0.7 %copy-start.3 = (s32[4,2,2]{0,2,1:T(2,128)S(1)}, s32[4,2,2]{0,2,1:T(2,128)}, u32[]{:S(2)}) copy-start(s32[4,2,2]{0,2,1:T(2,128)} %param.5) | copy-start | bytes 196
  0.0 0.8 %copy-start.2 = (s32[1024]{0:T(1024)S(1)}, s32[1024]{0:T(1024)}, u32[]{:S(2)}) copy-start(s32[1024]{0:T(1024)} %param.7) | copy-start | bytes 12292
  0.0 0.8 %copy-start.1 = (s32[1024]{0:T(1024)S(1)}, s32[1024]{0:T(1024)}, u32[]{:S(2)}) copy-start(s32[1024]{0:T(1024)} %param.6) | copy-start | bytes 12292
  0.8 1.2 %copy-start = (f32[4,32,2,1024]{3,2,1,0:T(2,128)S(1)}, f32[4,32,2,1024]{3,2,1,0:T(2,128)}, u32[]{:S(2)}) copy-start(f32[4,32,2,1024]{3,2,1,0:T(2,128)} %param.4) | copy-start | bytes 3145732
